TPU v7x, 32 devices: a whole 2x2x4 slice. The times are simulated.
32 devices in a mesh: date: 8 (over y, x, core), tile: 4 (over z).
Axes of the slice: x: 2, y: 2, z: 4, core: 2. Of those that a mesh axis runs over, the one named last changes fastest.
Arguments:
- reflectance: bfloat16 [2, 1024, 32, 512], P(None, 'date', 'tile'), may hold values from -6 to 6
- clear_sky: int32 [1024, 32, 4], P('date', 'tile'), may hold values 0 or 1
- harmonics: int32 [256], replicated, may hold values from 1 to 511, as said below
Outputs:
- anomaly: float32 [2, 1024, 32, 512], P(None, 'date', 'tile')
Inputs may be any that keep to these rules, and one draw needn't show every extreme that they name: `harmonics`: 256 distinct frequencies; 1 and 511 are always among them.
All inputs are finite; a program needn't handle non-finite values. No bound on the sum of `clear_sky` on one device may be relied on, other than what follows from the above.
Results may differ from a plain program's by a relative error of at most 0.0012.
Values may be sent and summed in bfloat16 or wider, within the bound.
No kernel may reach another device: no remote copies, remote signals or barrier semaphores. Data moves between devices by JAX's collectives and lax.ppermute only.
A program may use at most 64 MiB of HBM per device.

v0:
```python
import functools
import math

import jax
import jax.numpy as jnp
from jax import lax
from jax.experimental import pallas as pl
from jax.experimental.pallas import tpu as pltpu
from jax.sharding import PartitionSpec as P

LANES = 128
SUB = 32
MIB = 2**20
DATE, TILE = ("date", "tile")


def padded(size):
    return -(-size // LANES) * LANES


def turn_flags(clear_ref, flags_in, flags):
    height, blocks, dates = clear_ref.shape
    flags_in[...] = jnp.zeros_like(flags_in)
    for q in range(height):
        flags_in[q * blocks : (q + 1) * blocks, 0:dates] = clear_ref[q].astype(jnp.float32)
    flags[...] = flags_in[...].T.astype(jnp.bfloat16)


def grid_of(shape):
    return lax.broadcasted_iota(jnp.int32, shape, 0), lax.broadcasted_iota(jnp.int32, shape, 1)


def table_of(index, values):
    out = jnp.zeros_like(index)
    for i, value in enumerate(values):
        out = jnp.where(index == i, value, out)
    return out


def as_matrix(choice):
    return jnp.where(choice, 1.0, 0.0).astype(jnp.bfloat16)


def product(left, right):
    return jnp.dot(left, right, preferred_element_type=jnp.float32)


def add_row(lines, place, extra):
    parts = [lines[i : i + SUB] for i in range(0, lines.shape[0], SUB)]
    parts[place] = parts[place] + extra
    return jnp.concatenate(parts, axis=0)


def cover_matrices(height, blocks, width):
    line, date = grid_of((SUB * height, SUB))
    repeat = as_matrix(lax.div(line, height) == date)
    line, lane = grid_of((SUB * height, width))
    own = lax.rem(line, height) == lax.div(lane, blocks)
    lane, column = grid_of((width, blocks * LANES))
    columns = as_matrix(lax.rem(lane, blocks) == lax.div(column, LANES))
    return repeat, own, columns


def box_columns(blocks, width):
    lane, column = grid_of((width, blocks * LANES))
    total = jnp.zeros(lane.shape, jnp.float32)
    for shift in (-1, 0, 1):
        at = column + shift
        there = jnp.where(at < 0, -1, lax.div(at, LANES))
        total = total + jnp.where(there == lax.rem(lane, blocks), 1.0, 0.0)
    return total.astype(jnp.bfloat16)


def flag_lines(clear, repeat, own):
    return jnp.where(own, product(repeat, clear), 0.0).astype(jnp.bfloat16)


def turn_matrix(rows, height):
    line, source = grid_of((len(rows) * SUB, SUB * height))
    apart = jnp.abs(table_of(lax.div(line, SUB), rows) - lax.rem(source, height))
    return as_matrix((lax.rem(line, SUB) == lax.div(source, height)) & (apart <= 1))


def back_matrix(rows, height):
    line, source = grid_of((SUB * height, len(rows) * SUB))
    row = table_of(lax.div(source, SUB), rows)
    return as_matrix((lax.div(line, height) == lax.rem(source, SUB)) & (lax.rem(line, height) == row))


class Shelf:
    def __init__(self, rows, height, blocks, dates):
        width = padded(height * blocks)
        lines = len(rows) * SUB
        start = dates * height
        self.box = (pl.ds(start, width), pl.ds(0, blocks * LANES))
        start += width
        self.near = [(pl.ds(start + step * lines, lines), pl.ds(0, width)) for step in range(dates // SUB)]
        self.turn = (pl.ds(start, lines), pl.ds(width, SUB * height))
        self.back = (pl.ds(start + lines, SUB * height), pl.ds(width, SUB * height))
        self.size = start + max(dates // SUB * lines, lines + SUB * height)


def smooth_lines(down, scale, lane):
    cols = down.shape[1]
    west = jnp.where(lane == 0, 0.0, pltpu.roll(down, 1, 1))
    east = jnp.where(lane == cols - 1, 0.0, pltpu.roll(down, cols - 1, 1))
    return ((down + west + east) * scale).astype(jnp.bfloat16)


def file_lines(table, at, smoothed, rows, b, bands):
    blocks = smoothed.shape[1] // LANES
    for k in range(blocks):
        for i in range(len(rows)):
            part = smoothed[i * SUB : (i + 1) * SUB, k * LANES : (k + 1) * LANES]
            table[(k * len(rows) + i) * bands + b, at, :] = part


def give_pieces(table, pieces):
    units = table.shape[0] // len(pieces)
    chip = lax.axis_index(DATE) // 2
    for m, piece in enumerate(pieces):
        piece[...] = table[pl.ds((chip ^ m) * units, units)]


def first_kernel(chunks, chips, refl_ref, clear_ref, *refs):
    pieces, refs = refs[:chips], refs[chips:]
    masked_ref, first_ref, last_ref = refs[:3]
    table, held_ref, clear_held, flags_in, flags, sems = refs[3:]
    rows, rest = chunks
    bands, lines_all, cols = refl_ref.shape
    dates = pieces[0].shape[1]
    height = lines_all // dates
    shelf_ref = masked_ref.at[bands]
    blocks = cols // LANES
    flat = bands * blocks
    width = flags.shape[1]
    shelf = Shelf(rest, height, blocks, dates)

    def fetch(step):
        at = pl.ds(step * SUB * height, SUB * height)
        return pltpu.make_async_copy(refl_ref.at[:, at], held_ref.at[:, at], sems.at[step])

    fetch_clear = pltpu.make_async_copy(clear_ref, clear_held, sems.at[dates // SUB])
    fetch_clear.start()
    for step in range(dates // SUB):
        fetch(step).start()
    line, source = grid_of((2 * SUB, SUB * height))
    edge = jnp.where(line < SUB, 0, height - 1)
    edges = as_matrix((lax.rem(line, SUB) == lax.div(source, height)) & (edge == lax.rem(source, height)))
    flag_lane = lax.broadcasted_iota(jnp.int32, (SUB, width), 1)
    repeat, own, columns = cover_matrices(height, blocks, width)
    box = box_columns(blocks, width)
    turn = turn_matrix(rows, height)
    turn_rest = turn_matrix(rest, height)
    shelf_ref[shelf.box] = box
    shelf_ref[shelf.turn] = turn_rest
    shelf_ref[shelf.back] = back_matrix(rows + rest, height)
    lane = lax.broadcasted_iota(jnp.int32, (len(rows) * SUB, cols), 1)
    fetch_clear.wait()
    turn_flags(clear_held, flags_in, flags)

    for step in range(dates // SUB):
        at = pl.ds(step * SUB, SUB)
        here = pl.ds(step * SUB * height, SUB * height)
        clear = flags[at, :]
        lines = flag_lines(clear, repeat, own)
        cover = product(lines, columns).astype(jnp.bfloat16)
        shelf_ref[here, :] = cover
        for q, ref in ((0, first_ref), (height - 1, last_ref)):
            kept = jnp.where(lax.div(flag_lane, blocks) == q, clear.astype(jnp.float32), 0.0)
            ref[flat, at, :] = kept.astype(jnp.bfloat16)
        shelf_ref[shelf.near[step]] = product(turn_rest, lines).astype(jnp.bfloat16)
        count = product(product(turn, lines).astype(jnp.bfloat16), box)
        scale = 1.0 / jnp.maximum(count, 1.0)
        fetch(step).wait()
        for b in range(bands):
            masked = held_ref[b, here, :] * cover
            masked_ref[b, here, :] = masked
            ends = product(edges, masked).astype(jnp.bfloat16)
            for i, ref in enumerate((first_ref, last_ref)):
                for k in range(blocks):
                    ref[b * blocks + k, at, :] = ends[i * SUB : (i + 1) * SUB, k * LANES : (k + 1) * LANES]
            file_lines(table, at, smooth_lines(product(turn, masked), scale, lane), rows, b, bands)
    give_pieces(table, pieces)


def smooth_first(refl, clear, chunks, chips):
    bands, lines, cols = refl.shape
    height, blocks, dates = clear.shape
    number = bands * blocks * len(chunks[0])
    width = padded(height * blocks)
    pieces = [jax.ShapeDtypeStruct((number // chips, dates, LANES), jnp.bfloat16)] * chips
    size = Shelf(chunks[1], height, blocks, dates).size
    held = [pltpu.VMEM((bands + 1, size, cols), jnp.bfloat16)]
    edges = [jax.ShapeDtypeStruct((bands * blocks + 1, dates, width), jnp.bfloat16)] * 2
    return pl.pallas_call(
        functools.partial(first_kernel, chunks, chips),
        in_specs=[pl.BlockSpec(memory_space=pltpu.HBM)] * 2,
        out_specs=[pl.BlockSpec(memory_space=pltpu.VMEM)] * (chips + 3),
        out_shape=pieces + held + edges,
        scratch_shapes=[
            pltpu.VMEM((number, dates, LANES), jnp.bfloat16),
            pltpu.VMEM(refl.shape, refl.dtype),
            pltpu.VMEM(clear.shape, clear.dtype),
            pltpu.VMEM((width, padded(dates)), jnp.float32),
            pltpu.VMEM((padded(dates), width), jnp.bfloat16),
            pltpu.SemaphoreType.DMA((dates // SUB + 1,)),
        ],
        compiler_params=pltpu.CompilerParams(vmem_limit_bytes=14 * MIB),
        name="smooth_first",
    )(pltpu.with_memory_space_constraint(refl, pltpu.HBM), pltpu.with_memory_space_constraint(clear, pltpu.HBM))


def rest_kernel(rows, chips, height, masked_ref, before_ref, after_ref, *refs):
    pieces, table = refs[:chips], refs[chips]
    bands, cols = masked_ref.shape[0] - 1, masked_ref.shape[2]
    dates = pieces[0].shape[1]
    blocks = cols // LANES
    flat = bands * blocks
    shelf_ref = masked_ref.at[bands]
    shelf = Shelf(rows, height, blocks, dates)
    halo = tuple((rows.index(q), ref) for q, ref in ((0, before_ref), (height - 1, after_ref)))
    box, turn = shelf_ref[shelf.box], shelf_ref[shelf.turn]
    lane = lax.broadcasted_iota(jnp.int32, (len(rows) * SUB, cols), 1)
    for step in range(dates // SUB):
        at = pl.ds(step * SUB, SUB)
        here = pl.ds(step * SUB * height, SUB * height)
        count = product(shelf_ref[shelf.near[step]], box)
        for place, ref in halo:
            count = add_row(count, place, product(ref[flat, at, :], box))
        scale = 1.0 / jnp.maximum(count, 1.0)
        for b in range(bands):
            down = product(turn, masked_ref[b, here, :])
            for place, ref in halo:
                extra = jnp.concatenate([ref[b * blocks + k, at, :] for k in range(blocks)], axis=1)
                down = add_row(down, place, extra.astype(jnp.float32))
            file_lines(table, at, smooth_lines(down, scale, lane), rows, b, bands)
    give_pieces(table, pieces)


def hand_on_kernel(first_in, last_in, first_out, last_out):
    first_out[...] = first_in[...]
    last_out[...] = last_in[...]


def hand_on(first, last):
    return pl.pallas_call(
        hand_on_kernel,
        out_shape=[jax.ShapeDtypeStruct(x.shape, x.dtype) for x in (first, last)],
        compiler_params=pltpu.CompilerParams(vmem_limit_bytes=8 * MIB),
        name="hand_on",
    )(first, last)


def smooth_rest(masked, height, halo, rows, chips):
    bands, cols = masked.shape[0] - 1, masked.shape[2]
    dates = halo[0].shape[1]
    number = bands * (cols // LANES) * len(rows)
    return pl.pallas_call(
        functools.partial(rest_kernel, rows, chips, height),
        in_specs=[pl.BlockSpec(memory_space=pltpu.VMEM)] * 3,
        out_shape=[jax.ShapeDtypeStruct((number // chips, dates, LANES), jnp.bfloat16)] * chips,
        scratch_shapes=[pltpu.VMEM((number, dates, LANES), jnp.bfloat16)],
        compiler_params=pltpu.CompilerParams(vmem_limit_bytes=12 * MIB),
        name="smooth_rest",
    )(masked, *halo)


def filter_kernel(dates, wave_ref, high_ref, low_ref):
    total = high_ref.shape[1]
    chips = total // dates // 2
    core = lax.axis_index(DATE) % 2
    wave = jnp.concatenate(
        [jnp.broadcast_to(wave_ref[a : a + 1, :], (dates, LANES)) for a in range(total // LANES)], axis=1
    )
    same = pltpu.roll(wave, 0, 1, stride=1, stride_axis=0)
    other = jnp.where(core == 0, pltpu.roll(same, total - dates, 1), pltpu.roll(same, dates, 1))
    for side, base in enumerate((same, other)):
        high = base.astype(jnp.bfloat16)
        low = (base - high.astype(jnp.float32)).astype(jnp.bfloat16)
        for ref, part in ((high_ref, high), (low_ref, low)):
            for q in range(chips):
                for s in range(chips):
                    at = (s - q) % chips * 2 * dates
                    left = (side * chips + s) * dates
                    ref[q * dates : (q + 1) * dates, left : left + dates] = part[:, at : at + dates]


def filter_matrix(harmonics, dates, peers):
    total = dates * peers
    fine = jnp.arange(LANES, dtype=jnp.int32)
    coarse = jnp.arange(0, total, LANES, dtype=jnp.int32)

    def turned(steps):
        angle = (harmonics[:, None] * steps[None, :] % total).astype(jnp.float32) * (2.0 * math.pi / total)
        return jnp.cos(angle), jnp.sin(angle)

    (cos_a, sin_a), (cos_b, sin_b) = turned(coarse), turned(fine)
    wave = jnp.einsum(
        "fa,fb->ab",
        jnp.concatenate([cos_a, sin_a], axis=0),
        jnp.concatenate([cos_b, -sin_b], axis=0),
        precision=lax.Precision.HIGHEST,
    )
    wave = wave * (2.0 / total)
    return pl.pallas_call(
        functools.partial(filter_kernel, dates),
        out_shape=[jax.ShapeDtypeStruct((total // 2, total), jnp.bfloat16)] * 2,
        compiler_params=pltpu.CompilerParams(vmem_limit_bytes=10 * MIB),
        name="filter_matrix",
    )(wave)


def pack_kernel(chips, *refs):
    pieces, out_ref = refs[:chips], refs[-1]
    units, dates, lanes = pieces[0].shape
    chip = lax.axis_index(DATE) // 2
    for m in range(chips):
        at = pl.multiple_of((chip ^ m) * dates, dates)
        for i in range(units):
            out_ref[pl.ds(at, dates), i * lanes : (i + 1) * lanes] = pieces[m][i]


def pack(pieces, after):
    units, dates, lanes = pieces[0].shape
    return pl.pallas_call(
        functools.partial(pack_kernel, len(pieces)),
        out_shape=jax.ShapeDtypeStruct((len(pieces) * dates, units * lanes), jnp.bfloat16),
        in_specs=[pl.BlockSpec(memory_space=pltpu.VMEM)] * len(pieces) + [pl.BlockSpec(memory_space=pl.ANY)] * len(after),
        compiler_params=pltpu.CompilerParams(vmem_limit_bytes=8 * MIB),
        name="pack",
    )(*pieces, *after)


def apply_kernel(chips, high_ref, low_ref, own_ref, other_ref, *refs):
    outs, result = refs[:chips], refs[chips]
    units, dates, lanes = outs[0].shape
    half = own_ref.shape[0]
    chip = lax.axis_index(DATE) // 2
    tile = min(half, 256)

    @pl.loop(0, half // tile)
    def _(step):
        at = pl.ds(pl.multiple_of(step * tile, tile), tile)
        total = None
        for ref in (high_ref, low_ref):
            for series, left in ((own_ref, 0), (other_ref, half)):
                part = jnp.dot(
                    ref[at, left : left + half], series[...], preferred_element_type=jnp.float32
                )
                total = part if total is None else total + part
        result[at, :] = total

    for m in range(chips):
        at = pl.multiple_of((chip ^ m) * dates, dates)
        for i in range(units):
            outs[m][i] = result[pl.ds(at, dates), i * lanes : (i + 1) * lanes].astype(jnp.bfloat16)


def apply_filter(high, low, own, other, chips):
    half, width = own.shape
    piece = jax.ShapeDtypeStruct((width // LANES, half // chips, LANES), jnp.bfloat16)
    return pl.pallas_call(
        functools.partial(apply_kernel, chips),
        out_shape=[piece] * chips,
        scratch_shapes=[pltpu.VMEM((half, width), jnp.float32)],
        compiler_params=pltpu.CompilerParams(vmem_limit_bytes=16 * MIB),
        name="apply_filter",
    )(high, low, own, other)


def anomaly_kernel(chunks, chips, masked_ref, *refs):
    count = len(chunks) * chips
    pieces, (out_ref, table, made, sems) = refs[:count], refs[count:]
    bands, lines, cols = made.shape
    shelf_ref = masked_ref.at[bands]
    dates = table.shape[1]
    height = lines // dates
    blocks = cols // LANES
    chip = lax.axis_index(DATE) // 2
    order, start = [], 0
    for c, rows in enumerate(chunks):
        units = pieces[c * chips].shape[0]
        for m in range(chips):
            table[pl.ds(start + (chip ^ m) * units, units)] = pieces[c * chips + m][...]
        order += [(r, start + i * bands, len(rows) * bands) for i, r in enumerate(rows)]
        start += units * chips

    turn = shelf_ref[Shelf(chunks[1], height, blocks, dates).back]

    def store(step, b):
        here = pl.ds(step * SUB * height, SUB * height)
        return pltpu.make_async_copy(made.at[b, here], out_ref.at[b, here], sems.at[step, b])

    for step in range(dates // SUB):
        at = pl.ds(step * SUB, SUB)
        here = pl.ds(step * SUB * height, SUB * height)
        cover = shelf_ref[here, :].astype(jnp.float32)
        for b in range(bands):
            seasonal = jnp.concatenate(
                [
                    jnp.concatenate([table[first + k * step_k + b, at, :] for k in range(blocks)], axis=1)
                    for _, first, step_k in order
                ],
                axis=0,
            )
            made[b, here, :] = masked_ref[b, here, :].astype(jnp.float32) - cover * product(turn, seasonal)
            store(step, b).start()
    for step in range(dates // SUB):
        for b in range(bands):
            store(step, b).wait()


def anomaly(masked, height, chunks, pieces, chips):
    bands, cols = masked.shape[0] - 1, masked.shape[2]
    dates = pieces[0].shape[1]
    lines = dates * height
    return pl.pallas_call(
        functools.partial(anomaly_kernel, chunks, chips),
        in_specs=[pl.BlockSpec(memory_space=pltpu.VMEM)] * (1 + len(pieces)),
        out_specs=pl.BlockSpec(memory_space=pl.ANY),
        out_shape=jax.ShapeDtypeStruct((bands, lines, cols), jnp.float32),
        scratch_shapes=[
            pltpu.VMEM((bands * cols // LANES * height, dates, LANES), jnp.bfloat16),
            pltpu.VMEM((bands, lines, cols), jnp.float32),
            pltpu.SemaphoreType.DMA((dates // SUB, bands)),
        ],
        compiler_params=pltpu.CompilerParams(vmem_limit_bytes=16 * MIB),
        name="anomaly",
    )(masked, *pieces)


def exchange(pieces, peers):
    out = list(pieces)
    for m in range(len(pieces) - 1, 0, -1):
        out[m] = lax.ppermute(pieces[m], DATE, [(i, i ^ (2 * m)) for i in range(peers)])
    return out


def on_device(reflectance, clear_sky, harmonics):
    bands, dates, height, cols = reflectance.shape
    peers, tiles = lax.axis_size(DATE), lax.axis_size(TILE)
    chips = peers // 2
    clear = jnp.transpose(clear_sky, (1, 2, 0))
    chunks = (tuple(range(1, height - 1)), (height - 1, 0))
    refl = reflectance.reshape(bands, dates * height, cols)
    out = smooth_first(refl, clear, chunks, chips)
    masked, first, last = out[chips:]
    inner = exchange(out[:chips], peers)
    first, last = hand_on(first, last)
    up = [(i, i + 1) for i in range(tiles - 1)]
    before = lax.ppermute(last, TILE, up)
    after = lax.ppermute(first, TILE, [(j, i) for i, j in up])
    edges = smooth_rest(masked, height, (before, after), chunks[1], chips)
    outer = exchange(edges, peers)
    high, low = filter_matrix(harmonics, dates, peers)
    results, after = [], [high, edges[0]]
    for pieces in (inner, outer):
        own = pack(pieces, after)
        other = lax.ppermute(own, DATE, [(i, i ^ 1) for i in range(peers)])
        made = apply_filter(high, low, own, other, chips)
        results += exchange(made, peers)
        after = [made[0]]
    return anomaly(masked, height, chunks, results, chips).reshape(reflectance.shape)


def solution(mesh):
    return jax.shard_map(
        on_device,
        mesh=mesh,
        in_specs=(P(None, DATE, TILE, None), P(DATE, TILE, None), P()),
        out_specs=P(None, DATE, TILE, None),
        check_vma=False,
    )
```

profile of v0, /device:TPU:0, one launch (start us, length us, event | category | flops | bytes accessed | tf_op | source)
XLA Modules:
  0.0 65.2 jit_solution(11830535233369741251)
XLA Ops:
  0.0 4.4 %smooth_first.1 = (bf16[12,128,128]{2,1,0:T(8,128)(2,1)S(1)}, bf16[12,128,128]{2,1,0:T(8,128)(2,1)S(1)}, bf16[12,128,128]{2,1,0:T(8,128)(2,1)S(1)}, bf16[12,128,...) custom-call(bf16[2,1024,512]{2,1,0:T(8,128)(2,1)} %bitcast.3, ...), custom_call_target="tpu_custom_call" | custom-call | tf_op jit(solution)/shard_map/smooth_first/pallas_call | solution.py:196
  4.4 3.0 %collective-permute-start = (bf16[12,128,128]{2,1,0:T(8,128)(2,1)S(1)}, bf16[12,128,128]{2,1,0:T(8,128)(2,1)S(1)}, u32[]{:S(2)}, u32[]{:S(2)}) collective-permute-start(bf16[12,128,128]{2,1,0:T(8,128)(2,1)S(1)} %get-tuple-element.32), channel_id=1, source_target_pairs={{0,8},{4,12},{8,0},{12,4},{16,24},{20,28},{24,16},{28,20},{1,9},{5... | collective-permute-start | bytes 1179656 | tf_op jit(solution)/shard_map/ppermute | solution.py:436
  7.4 1.5 %collective-permute-start.1 = (bf16[12,128,128]{2,1,0:T(8,128)(2,1)S(1)}, bf16[12,128,128]{2,1,0:T(8,128)(2,1)S(1)}, u32[]{:S(2)}, u32[]{:S(2)}) collective-permute-start(bf16[12,128,128]{2,1,0:T(8,128)(2,1)S(1)} %get-tuple-element.33), channel_id=1, source_target_pairs={{0,16},{4,20},{8,24},{12,28},{16,0},{20,4},{24,8},{28,12},{1,17},{... | collective-permute-start | bytes 1179656 | tf_op jit(solution)/shard_map/ppermute | solution.py:436
  9.0 4.0 %collective-permute-start.3 = (bf16[9,128,128]{2,1,0:T(8,128)(2,1)S(1)}, bf16[9,128,128]{2,1,0:T(8,128)(2,1)S(1)}, u32[]{:S(2)}, u32[]{:S(2)}) collective-permute-start(bf16[9,128,128]{2,1,0:T(8,128)(2,1)S(1)} %get-tuple-element.37), channel_id=1, source_target_pairs={{0,1},{1,2},{2,3},{4,5},{5,6},{6,7},{8,9},{9,10},{10,11},{12,13},{... | collective-permute-start | bytes 884744 | tf_op jit(solution)/shard_map/ppermute | solution.py:452
  13.0 1.3 %collective-permute-start.4 = (bf16[9,128,128]{2,1,0:T(8,128)(2,1)S(1)}, bf16[9,128,128]{2,1,0:T(8,128)(2,1)S(1)}, u32[]{:S(2)}, u32[]{:S(2)}) collective-permute-start(bf16[9,128,128]{2,1,0:T(8,128)(2,1)S(1)} %get-tuple-element.38), channel_id=1, source_target_pairs={{1,0},{2,1},{3,2},{5,4},{6,5},{7,6},{9,8},{10,9},{11,10},{13,12},{... | collective-permute-start | bytes 884744 | tf_op jit(solution)/shard_map/ppermute | solution.py:453
  15.6 2.7 %collective-permute-done.3.before_ref = bf16[9,128,128]{2,1,0:T(8,128)(2,1)S(1)} collective-permute-done((bf16[9,128,128]{2,1,0:T(8,128)(2,1)S(1)}, bf16[9,128,128]{2,1,0:T(8,128)(2,1)S(1)}, u32[]{:S(2)}, u32[]{:S(2)}) %collective-permute-start.3) | collective-permute-done | bytes 294944 | tf_op jit(solution)/shard_map/ppermute | solution.py:452
  18.4 4.1 %collective-permute-done.4.after_ref = bf16[9,128,128]{2,1,0:T(8,128)(2,1)S(1)} collective-permute-done((bf16[9,128,128]{2,1,0:T(8,128)(2,1)S(1)}, bf16[9,128,128]{2,1,0:T(8,128)(2,1)S(1)}, u32[]{:S(2)}, u32[]{:S(2)}) %collective-permute-start.4) | collective-permute-done | bytes 294944 | tf_op jit(solution)/shard_map/ppermute | solution.py:453
  22.5 1.0 %smooth_rest.1 = (bf16[4,128,128]{2,1,0:T(8,128)(2,1)S(1)}, bf16[4,128,128]{2,1,0:T(8,128)(2,1)S(1)}, bf16[4,128,128]{2,1,0:T(8,128)(2,1)S(1)}, bf16[4,128,128]{2,1,0:T(8,128)(2,1)S(1)}) custom-call(bf16[3,1472,512]{2,1,0:T(8,128)(2,1)S(1)} %get-tuple-element.28.masked_ref, bf16[9,128,128]{2,1,0:T(8,128)(2,1)S(1)} %collective-permute-done.3.before_ref, ...), custom_call_target="tpu_custom_call" | custom-call | tf_op jit(solution)/shard_map/smooth_rest/pallas_call | solution.py:259
  23.5 2.9 %collective-permute-done.1.refs_2_ = bf16[12,128,128]{2,1,0:T(8,128)(2,1)S(1)} collective-permute-done((bf16[12,128,128]{2,1,0:T(8,128)(2,1)S(1)}, bf16[12,128,128]{2,1,0:T(8,128)(2,1)S(1)}, u32[]{:S(2)}, u32[]{:S(2)}) %collective-permute-start.1) | collective-permute-done | bytes 393248 | tf_op jit(solution)/shard_map/ppermute | solution.py:436
  26.8 1.3 %collective-permute-start.9 = (bf16[4,128,128]{2,1,0:T(8,128)(2,1)S(1)}, bf16[4,128,128]{2,1,0:T(8,128)(2,1)S(1)}, u32[]{:S(2)}, u32[]{:S(2)}) collective-permute-start(bf16[4,128,128]{2,1,0:T(8,128)(2,1)S(1)} %get-tuple-element.44), channel_id=1, source_target_pairs={{0,8},{4,12},{8,0},{12,4},{16,24},{20,28},{24,16},{28,20},{1,9},{5... | collective-permute-start | bytes 393224 | tf_op jit(solution)/shard_map/ppermute | solution.py:436
  28.9 1.4 %collective-permute-start.11 = (bf16[4,128,128]{2,1,0:T(8,128)(2,1)S(1)}, bf16[4,128,128]{2,1,0:T(8,128)(2,1)S(1)}, u32[]{:S(2)}, u32[]{:S(2)}) collective-permute-start(bf16[4,128,128]{2,1,0:T(8,128)(2,1)S(1)} %get-tuple-element.46), channel_id=1, source_target_pairs={{0,24},{4,28},{8,16},{12,20},{16,8},{20,12},{24,0},{28,4},{1,25},{... | collective-permute-start | bytes 393224 | tf_op jit(solution)/shard_map/ppermute | solution.py:436
  30.3 3.7 %apply_filter.2 = (bf16[12,128,128]{2,1,0:T(8,128)(2,1)S(1)}, bf16[12,128,128]{2,1,0:T(8,128)(2,1)S(1)}, bf16[12,128,128]{2,1,0:T(8,128)(2,1)S(1)}, bf16[12,128,128]{2,1,0:T(8,128)(2,1)S(1)}) custom-call(bf16[512,1024]{1,0:T(8,128)(2,1)S(1)} %get-tuple-element.29.refs_4_.high_ref, bf16[512,1024]{1,0:T(8,128)(2,1)S(1)} %get-tuple-element.30.low_ref, ...), custom_call_target="tpu_custom_call" | custom-call | tf_op jit(solution)/shard_map/apply_filter/pallas_call | solution.py:363
  34.8 1.6 %collective-permute-done.11.refs_3_ = bf16[4,128,128]{2,1,0:T(8,128)(2,1)S(1)} collective-permute-done((bf16[4,128,128]{2,1,0:T(8,128)(2,1)S(1)}, bf16[4,128,128]{2,1,0:T(8,128)(2,1)S(1)}, u32[]{:S(2)}, u32[]{:S(2)}) %collective-permute-start.11) | collective-permute-done | bytes 131104 | tf_op jit(solution)/shard_map/ppermute | solution.py:436
  37.5 1.5 %collective-permute-start.7 = (bf16[12,128,128]{2,1,0:T(8,128)(2,1)S(1)}, bf16[12,128,128]{2,1,0:T(8,128)(2,1)S(1)}, u32[]{:S(2)}, u32[]{:S(2)}) collective-permute-start(bf16[12,128,128]{2,1,0:T(8,128)(2,1)S(1)} %get-tuple-element.42), channel_id=1, source_target_pairs={{0,16},{4,20},{8,24},{12,28},{16,0},{20,4},{24,8},{28,12},{1,17},{... | collective-permute-start | bytes 1179656 | tf_op jit(solution)/shard_map/ppermute | solution.py:436
  39.0 1.2 %collective-permute-start.8 = (bf16[12,128,128]{2,1,0:T(8,128)(2,1)S(1)}, bf16[12,128,128]{2,1,0:T(8,128)(2,1)S(1)}, u32[]{:S(2)}, u32[]{:S(2)}) collective-permute-start(bf16[12,128,128]{2,1,0:T(8,128)(2,1)S(1)} %get-tuple-element.43), channel_id=1, source_target_pairs={{0,24},{4,28},{8,16},{12,20},{16,8},{20,12},{24,0},{28,4},{1,25},{... | collective-permute-start | bytes 1179656 | tf_op jit(solution)/shard_map/ppermute | solution.py:436
  40.2 1.5 %apply_filter.3 = (bf16[4,128,128]{2,1,0:T(8,128)(2,1)S(1)}, bf16[4,128,128]{2,1,0:T(8,128)(2,1)S(1)}, bf16[4,128,128]{2,1,0:T(8,128)(2,1)S(1)}, bf16[4,128,128]{2,1,0:T(8,128)(2,1)S(1)}) custom-call(bf16[512,1024]{1,0:T(8,128)(2,1)S(1)} %get-tuple-element.29.refs_4_.high_ref, bf16[512,1024]{1,0:T(8,128)(2,1)S(1)} %get-tuple-element.30.low_ref, ...), custom_call_target="tpu_custom_call" | custom-call | tf_op jit(solution)/shard_map/apply_filter/pallas_call | solution.py:363
  41.7 0.9 %collective-permute-start.13 = (bf16[4,128,128]{2,1,0:T(8,128)(2,1)S(1)}, bf16[4,128,128]{2,1,0:T(8,128)(2,1)S(1)}, u32[]{:S(2)}, u32[]{:S(2)}) collective-permute-start(bf16[4,128,128]{2,1,0:T(8,128)(2,1)S(1)} %get-tuple-element.48), channel_id=1, source_target_pairs={{0,8},{4,12},{8,0},{12,4},{16,24},{20,28},{24,16},{28,20},{1,9},{5... | collective-permute-start | bytes 393224 | tf_op jit(solution)/shard_map/ppermute | solution.py:436
  42.5 1.5 %collective-permute-start.14 = (bf16[4,128,128]{2,1,0:T(8,128)(2,1)S(1)}, bf16[4,128,128]{2,1,0:T(8,128)(2,1)S(1)}, u32[]{:S(2)}, u32[]{:S(2)}) collective-permute-start(bf16[4,128,128]{2,1,0:T(8,128)(2,1)S(1)} %get-tuple-element.49), channel_id=1, source_target_pairs={{0,16},{4,20},{8,24},{12,28},{16,0},{20,4},{24,8},{28,12},{1,17},{... | collective-permute-start | bytes 393224 | tf_op jit(solution)/shard_map/ppermute | solution.py:436
  44.1 4.6 %collective-permute-done.6.refs_1_ = bf16[12,128,128]{2,1,0:T(8,128)(2,1)S(1)} collective-permute-done((bf16[12,128,128]{2,1,0:T(8,128)(2,1)S(1)}, bf16[12,128,128]{2,1,0:T(8,128)(2,1)S(1)}, u32[]{:S(2)}, u32[]{:S(2)}) %collective-permute-start.6) | collective-permute-done | bytes 393248 | tf_op jit(solution)/shard_map/ppermute | solution.py:436
  48.6 1.8 %collective-permute-start.15 = (bf16[4,128,128]{2,1,0:T(8,128)(2,1)S(1)}, bf16[4,128,128]{2,1,0:T(8,128)(2,1)S(1)}, u32[]{:S(2)}, u32[]{:S(2)}) collective-permute-start(bf16[4,128,128]{2,1,0:T(8,128)(2,1)S(1)} %get-tuple-element.50), channel_id=1, source_target_pairs={{0,24},{4,28},{8,16},{12,20},{16,8},{20,12},{24,0},{28,4},{1,25},{... | collective-permute-start | bytes 393224 | tf_op jit(solution)/shard_map/ppermute | solution.py:436
  50.4 7.5 %collective-permute-done.7.refs_2_ = bf16[12,128,128]{2,1,0:T(8,128)(2,1)S(1)} collective-permute-done((bf16[12,128,128]{2,1,0:T(8,128)(2,1)S(1)}, bf16[12,128,128]{2,1,0:T(8,128)(2,1)S(1)}, u32[]{:S(2)}, u32[]{:S(2)}) %collective-permute-start.7) | collective-permute-done | bytes 393248 | tf_op jit(solution)/shard_map/ppermute | solution.py:436
  57.9 2.0 %collective-permute-done.13.refs_5_ = bf16[4,128,128]{2,1,0:T(8,128)(2,1)S(1)} collective-permute-done((bf16[4,128,128]{2,1,0:T(8,128)(2,1)S(1)}, bf16[4,128,128]{2,1,0:T(8,128)(2,1)S(1)}, u32[]{:S(2)}, u32[]{:S(2)}) %collective-permute-start.13) | collective-permute-done | bytes 131104 | tf_op jit(solution)/shard_map/ppermute | solution.py:436
  59.9 2.8 %collective-permute-done.14.refs_6_ = bf16[4,128,128]{2,1,0:T(8,128)(2,1)S(1)} collective-permute-done((bf16[4,128,128]{2,1,0:T(8,128)(2,1)S(1)}, bf16[4,128,128]{2,1,0:T(8,128)(2,1)S(1)}, u32[]{:S(2)}, u32[]{:S(2)}) %collective-permute-start.14) | collective-permute-done | bytes 131104 | tf_op jit(solution)/shard_map/ppermute | solution.py:436
  62.7 2.5 %anomaly.1 = f32[2,1024,512]{2,1,0:T(8,128)} custom-call(bf16[3,1472,512]{2,1,0:T(8,128)(2,1)S(1)} %get-tuple-element.28.masked_ref, bf16[12,128,128]{2,1,0:T(8,128)(2,1)S(1)} %get-tuple-element.40.refs_4_.refs_0_, bf16[12,128,128]{2,1,0:T(8,128)(2,1)S(1)} %collective-permute-done.6.refs_1_, bf16[12,128,128]{2,1,0:T(8,128)(2,1)S(1)} %collective-permute-done.7.refs_2_, ...), custom_call_target="tpu_custom_call" | custom-call | tf_op jit(solution)/shard_map/anomaly/pallas_call | solution.py:418
  (23 shorter events, 4.3 us)
Async XLA Ops:
  0.0 14.3 %copy-start = (s32[256]{0:T(256)S(1)}, s32[256]{0:T(256)}, u32[]{:S(2)}) copy-start(s32[256]{0:T(256)} %param.5) | copy-start | bytes 3076
  4.4 19.1 %collective-permute-start = (bf16[12,128,128]{2,1,0:T(8,128)(2,1)S(1)}, bf16[12,128,128]{2,1,0:T(8,128)(2,1)S(1)}, u32[]{:S(2)}, u32[]{:S(2)}) collective-permute-start(bf16[12,128,128]{2,1,0:T(8,128)(2,1)S(1)} %get-tuple-element.32), channel_id=1, source_target_pairs={{0,8},{4,12},{8,0},{12,4},{16,24},{20,28},{24,16},{28,20},{1,9},{5... | collective-permute-start | bytes 1179656 | tf_op jit(solution)/shard_map/ppermute | solution.py:436
  7.4 19.0 %collective-permute-start.1 = (bf16[12,128,128]{2,1,0:T(8,128)(2,1)S(1)}, bf16[12,128,128]{2,1,0:T(8,128)(2,1)S(1)}, u32[]{:S(2)}, u32[]{:S(2)}) collective-permute-start(bf16[12,128,128]{2,1,0:T(8,128)(2,1)S(1)} %get-tuple-element.33), channel_id=1, source_target_pairs={{0,16},{4,20},{8,24},{12,28},{16,0},{20,4},{24,8},{28,12},{1,17},{... | collective-permute-start | bytes 1179656 | tf_op jit(solution)/shard_map/ppermute | solution.py:436
  8.9 17.5 %collective-permute-start.2 = (bf16[12,128,128]{2,1,0:T(8,128)(2,1)S(1)}, bf16[12,128,128]{2,1,0:T(8,128)(2,1)S(1)}, u32[]{:S(2)}, u32[]{:S(2)}) collective-permute-start(bf16[12,128,128]{2,1,0:T(8,128)(2,1)S(1)} %get-tuple-element.34), channel_id=1, source_target_pairs={{0,24},{4,28},{8,16},{12,20},{16,8},{20,12},{24,0},{28,4},{1,25},{... | collective-permute-start | bytes 1179656 | tf_op jit(solution)/shard_map/ppermute | solution.py:436
  9.0 9.4 %collective-permute-start.3 = (bf16[9,128,128]{2,1,0:T(8,128)(2,1)S(1)}, bf16[9,128,128]{2,1,0:T(8,128)(2,1)S(1)}, u32[]{:S(2)}, u32[]{:S(2)}) collective-permute-start(bf16[9,128,128]{2,1,0:T(8,128)(2,1)S(1)} %get-tuple-element.37), channel_id=1, source_target_pairs={{0,1},{1,2},{2,3},{4,5},{5,6},{6,7},{8,9},{9,10},{10,11},{12,13},{... | collective-permute-start | bytes 884744 | tf_op jit(solution)/shard_map/ppermute | solution.py:452
  13.0 9.5 %collective-permute-start.4 = (bf16[9,128,128]{2,1,0:T(8,128)(2,1)S(1)}, bf16[9,128,128]{2,1,0:T(8,128)(2,1)S(1)}, u32[]{:S(2)}, u32[]{:S(2)}) collective-permute-start(bf16[9,128,128]{2,1,0:T(8,128)(2,1)S(1)} %get-tuple-element.38), channel_id=1, source_target_pairs={{1,0},{2,1},{3,2},{5,4},{6,5},{7,6},{9,8},{10,9},{11,10},{13,12},{... | collective-permute-start | bytes 884744 | tf_op jit(solution)/shard_map/ppermute | solution.py:453
  26.7 3.6 %collective-permute-start.5 = (bf16[512,1536]{1,0:T(8,128)(2,1)S(1)}, bf16[512,1536]{1,0:T(8,128)(2,1)S(1)}, u32[]{:S(2)}, u32[]{:S(2)}) collective-permute-start(bf16[512,1536]{1,0:T(8,128)(2,1)S(1)} %pack.2.own_ref), channel_id=1, source_target_pairs={{0,4},{4,0},{8,12},{12,8},{16,20},{20,16},{24,28},{28,24},{1,5},{5... | collective-permute-start | bytes 4718600 | tf_op jit(solution)/shard_map/ppermute | solution.py:460
  26.8 7.3 %collective-permute-start.9 = (bf16[4,128,128]{2,1,0:T(8,128)(2,1)S(1)}, bf16[4,128,128]{2,1,0:T(8,128)(2,1)S(1)}, u32[]{:S(2)}, u32[]{:S(2)}) collective-permute-start(bf16[4,128,128]{2,1,0:T(8,128)(2,1)S(1)} %get-tuple-element.44), channel_id=1, source_target_pairs={{0,8},{4,12},{8,0},{12,4},{16,24},{20,28},{24,16},{28,20},{1,9},{5... | collective-permute-start | bytes 393224 | tf_op jit(solution)/shard_map/ppermute | solution.py:436
  28.1 6.8 %collective-permute-start.10 = (bf16[4,128,128]{2,1,0:T(8,128)(2,1)S(1)}, bf16[4,128,128]{2,1,0:T(8,128)(2,1)S(1)}, u32[]{:S(2)}, u32[]{:S(2)}) collective-permute-start(bf16[4,128,128]{2,1,0:T(8,128)(2,1)S(1)} %get-tuple-element.45), channel_id=1, source_target_pairs={{0,16},{4,20},{8,24},{12,28},{16,0},{20,4},{24,8},{28,12},{1,17},{... | collective-permute-start | bytes 393224 | tf_op jit(solution)/shard_map/ppermute | solution.py:436
  28.9 7.6 %collective-permute-start.11 = (bf16[4,128,128]{2,1,0:T(8,128)(2,1)S(1)}, bf16[4,128,128]{2,1,0:T(8,128)(2,1)S(1)}, u32[]{:S(2)}, u32[]{:S(2)}) collective-permute-start(bf16[4,128,128]{2,1,0:T(8,128)(2,1)S(1)} %get-tuple-element.46), channel_id=1, source_target_pairs={{0,24},{4,28},{8,16},{12,20},{16,8},{20,12},{24,0},{28,4},{1,25},{... | collective-permute-start | bytes 393224 | tf_op jit(solution)/shard_map/ppermute | solution.py:436
  36.6 3.6 %collective-permute-start.12 = (bf16[512,512]{1,0:T(8,128)(2,1)S(1)}, bf16[512,512]{1,0:T(8,128)(2,1)S(1)}, u32[]{:S(2)}, u32[]{:S(2)}) collective-permute-start(bf16[512,512]{1,0:T(8,128)(2,1)S(1)} %pack.3.own_ref), channel_id=1, source_target_pairs={{0,4},{4,0},{8,12},{12,8},{16,20},{20,16},{24,28},{28,24},{1,5},{5... | collective-permute-start | bytes 1572872 | tf_op jit(solution)/shard_map/ppermute | solution.py:460
  36.6 12.0 %collective-permute-start.6 = (bf16[12,128,128]{2,1,0:T(8,128)(2,1)S(1)}, bf16[12,128,128]{2,1,0:T(8,128)(2,1)S(1)}, u32[]{:S(2)}, u32[]{:S(2)}) collective-permute-start(bf16[12,128,128]{2,1,0:T(8,128)(2,1)S(1)} %get-tuple-element.41), channel_id=1, source_target_pairs={{0,8},{4,12},{8,0},{12,4},{16,24},{20,28},{24,16},{28,20},{1,9},{5... | collective-permute-start | bytes 1179656 | tf_op jit(solution)/shard_map/ppermute | solution.py:436
  37.5 20.4 %collective-permute-start.7 = (bf16[12,128,128]{2,1,0:T(8,128)(2,1)S(1)}, bf16[12,128,128]{2,1,0:T(8,128)(2,1)S(1)}, u32[]{:S(2)}, u32[]{:S(2)}) collective-permute-start(bf16[12,128,128]{2,1,0:T(8,128)(2,1)S(1)} %get-tuple-element.42), channel_id=1, source_target_pairs={{0,16},{4,20},{8,24},{12,28},{16,0},{20,4},{24,8},{28,12},{1,17},{... | collective-permute-start | bytes 1179656 | tf_op jit(solution)/shard_map/ppermute | solution.py:436
  39.0 18.9 %collective-permute-start.8 = (bf16[12,128,128]{2,1,0:T(8,128)(2,1)S(1)}, bf16[12,128,128]{2,1,0:T(8,128)(2,1)S(1)}, u32[]{:S(2)}, u32[]{:S(2)}) collective-permute-start(bf16[12,128,128]{2,1,0:T(8,128)(2,1)S(1)} %get-tuple-element.43), channel_id=1, source_target_pairs={{0,24},{4,28},{8,16},{12,20},{16,8},{20,12},{24,0},{28,4},{1,25},{... | collective-permute-start | bytes 1179656 | tf_op jit(solution)/shard_map/ppermute | solution.py:436
  41.7 18.2 %collective-permute-start.13 = (bf16[4,128,128]{2,1,0:T(8,128)(2,1)S(1)}, bf16[4,128,128]{2,1,0:T(8,128)(2,1)S(1)}, u32[]{:S(2)}, u32[]{:S(2)}) collective-permute-start(bf16[4,128,128]{2,1,0:T(8,128)(2,1)S(1)} %get-tuple-element.48), channel_id=1, source_target_pairs={{0,8},{4,12},{8,0},{12,4},{16,24},{20,28},{24,16},{28,20},{1,9},{5... | collective-permute-start | bytes 393224 | tf_op jit(solution)/shard_map/ppermute | solution.py:436
  42.5 20.2 %collective-permute-start.14 = (bf16[4,128,128]{2,1,0:T(8,128)(2,1)S(1)}, bf16[4,128,128]{2,1,0:T(8,128)(2,1)S(1)}, u32[]{:S(2)}, u32[]{:S(2)}) collective-permute-start(bf16[4,128,128]{2,1,0:T(8,128)(2,1)S(1)} %get-tuple-element.49), channel_id=1, source_target_pairs={{0,16},{4,20},{8,24},{12,28},{16,0},{20,4},{24,8},{28,12},{1,17},{... | collective-permute-start | bytes 393224 | tf_op jit(solution)/shard_map/ppermute | solution.py:436
  48.6 14.1 %collective-permute-start.15 = (bf16[4,128,128]{2,1,0:T(8,128)(2,1)S(1)}, bf16[4,128,128]{2,1,0:T(8,128)(2,1)S(1)}, u32[]{:S(2)}, u32[]{:S(2)}) collective-permute-start(bf16[4,128,128]{2,1,0:T(8,128)(2,1)S(1)} %get-tuple-element.50), channel_id=1, source_target_pairs={{0,24},{4,28},{8,16},{12,20},{16,8},{20,12},{24,0},{28,4},{1,25},{... | collective-permute-start | bytes 393224 | tf_op jit(solution)/shard_map/ppermute | solution.py:436
where the time goes:
time: 65.4 us; the launch traced here: 65.2 us
  waiting for transfers between devices  29.1 us (44%)
  starting transfers between devices  21.2 us (32%)
  Pallas kernels  13.8 us (21%)
  other arithmetic  0.72 us (1%)
    ppermute x12, waiting for transfers between devices, exchange(): lax.ppermute(pieces[m], DATE, [(i, i ^ 2 * m) for i in range(peers)])  22.3 us
    ppermute x12, starting transfers between devices, exchange(): lax.ppermute(pieces[m], DATE, [(i, i ^ 2 * m) for i in range(peers)])  15.8 us
    pallas_call x2, Pallas kernels, apply_filter(): pl.pallas_call(functools.partial(apply_kernel, chips), out_shape=[piece]...  5.19 us
    pallas_call x1, Pallas kernels, smooth_first(): pl.pallas_call(functools.partial(first_kernel, chunks, chips), in_specs=[...  4.4 us
    ppermute x1, waiting for transfers between devices, on_device(): after = lax.ppermute(first, TILE, [(j, i) for i, j in up])  4.13 us
    ppermute x1, starting transfers between devices, on_device(): before = lax.ppermute(last, TILE, up)  3.95 us
    ppermute x1, waiting for transfers between devices, on_device(): before = lax.ppermute(last, TILE, up)  2.74 us
    pallas_call x1, Pallas kernels, anomaly(): pl.pallas_call(functools.partial(anomaly_kernel, chunks, chips), in_specs...  2.47 us
  transfers between devices with their start and end apart: 16, of which 9 were waited for; matrix products, arithmetic and copies ran while one was open for 1% of the time, Pallas kernels for 10%

commit v1 on v0

--- a/solution.py
+++ b/solution.py
@@ -318,25 +318,30 @@
     for m in range(chips):
         at = pl.multiple_of((chip ^ m) * dates, dates)
         for i in range(units):
-            out_ref[pl.ds(at, dates), i * lanes : (i + 1) * lanes] = pieces[m][i]
-
-
-def pack(pieces, after):
+            part = (pl.ds(at, dates), pl.ds(i * lanes, lanes))
+            for side in ((0,), (1,)) if len(out_ref.shape) == 3 else ((),):
+                out_ref[side + part] = pieces[m][i]
+
+
+def pack(pieces, after, copies):
     units, dates, lanes = pieces[0].shape
+    shape = (len(pieces) * dates, units * lanes)
     return pl.pallas_call(
         functools.partial(pack_kernel, len(pieces)),
-        out_shape=jax.ShapeDtypeStruct((len(pieces) * dates, units * lanes), jnp.bfloat16),
-        in_specs=[pl.BlockSpec(memory_space=pltpu.VMEM)] * len(pieces) + [pl.BlockSpec(memory_space=pl.ANY)] * len(after),
+        in_specs=[pl.BlockSpec(memory_space=pltpu.VMEM)] * len(pieces)
+        + [pl.BlockSpec(memory_space=pl.ANY)] * len(after),
+        out_shape=jax.ShapeDtypeStruct((copies, *shape) if copies > 1 else shape, jnp.bfloat16),
         compiler_params=pltpu.CompilerParams(vmem_limit_bytes=8 * MIB),
         name="pack",
     )(*pieces, *after)
 
 
-def apply_kernel(chips, high_ref, low_ref, own_ref, other_ref, *refs):
-    outs, result = refs[:chips], refs[chips]
-    units, dates, lanes = outs[0].shape
-    half = own_ref.shape[0]
-    chip = lax.axis_index(DATE) // 2
+def apply_kernel(chips, shared, high_ref, low_ref, *refs):
+    outs, result = refs[-2] if shared else refs[-1 - chips : -1], refs[-1]
+    units, dates, lanes = outs.shape[1:] if shared else outs[0].shape
+    half = high_ref.shape[0]
+    chip, core = lax.axis_index(DATE) // 2, lax.axis_index(DATE) % 2
+    own_ref, other_ref = (refs[0].at[core], refs[0].at[1 - core]) if shared else refs[:2]
     tile = min(half, 256)
 
     @pl.loop(0, half // tile)
@@ -345,48 +350,60 @@
         total = None
         for ref in (high_ref, low_ref):
             for series, left in ((own_ref, 0), (other_ref, half)):
-                part = jnp.dot(
-                    ref[at, left : left + half], series[...], preferred_element_type=jnp.float32
-                )
+                part = product(ref[at, left : left + half], series[...])
                 total = part if total is None else total + part
         result[at, :] = total
 
     for m in range(chips):
-        at = pl.multiple_of((chip ^ m) * dates, dates)
+        at = m * dates if shared else pl.multiple_of((chip ^ m) * dates, dates)
+        out = outs.at[m] if shared else outs[m]
         for i in range(units):
-            outs[m][i] = result[pl.ds(at, dates), i * lanes : (i + 1) * lanes].astype(jnp.bfloat16)
-
-
-def apply_filter(high, low, own, other, chips):
-    half, width = own.shape
+            out[i] = result[pl.ds(at, dates), i * lanes : (i + 1) * lanes].astype(jnp.bfloat16)
+
+
+def apply_filter(high, low, series, chips):
+    half, width = series[0].shape[-2:]
     piece = jax.ShapeDtypeStruct((width // LANES, half // chips, LANES), jnp.bfloat16)
-    return pl.pallas_call(
-        functools.partial(apply_kernel, chips),
-        out_shape=[piece] * chips,
+    shared = len(series) == 1
+    return pl.pallas_call(
+        functools.partial(apply_kernel, chips, shared),
+        out_shape=jax.ShapeDtypeStruct((chips, *piece.shape), piece.dtype) if shared else [piece] * chips,
         scratch_shapes=[pltpu.VMEM((half, width), jnp.float32)],
         compiler_params=pltpu.CompilerParams(vmem_limit_bytes=16 * MIB),
         name="apply_filter",
-    )(high, low, own, other)
+    )(high, low, *series)
 
 
 def anomaly_kernel(chunks, chips, masked_ref, *refs):
-    count = len(chunks) * chips
-    pieces, (out_ref, table, made, sems) = refs[:count], refs[count:]
+    pieces, whole_ref, (out_ref, table, held, turn_held, made, sems) = refs[:chips], refs[chips], refs[chips + 1 :]
     bands, lines, cols = made.shape
-    shelf_ref = masked_ref.at[bands]
     dates = table.shape[1]
     height = lines // dates
     blocks = cols // LANES
     chip = lax.axis_index(DATE) // 2
+    turn_at, turn_cols = Shelf(chunks[1], height, blocks, dates).back
+    fetch_turn = pltpu.make_async_copy(masked_ref.at[bands, turn_at], turn_held, sems.at[0, bands + 1])
+
+    def fetch(step):
+        here = pl.ds(step * SUB * height, SUB * height)
+        return pltpu.make_async_copy(masked_ref.at[:, here], held.at[:, here], sems.at[step, bands])
+
+    fetch_turn.start()
+    for step in range(dates // SUB):
+        fetch(step).start()
     order, start = [], 0
     for c, rows in enumerate(chunks):
-        units = pieces[c * chips].shape[0]
+        units = whole_ref.shape[1] if c > 0 else pieces[0].shape[0]
         for m in range(chips):
-            table[pl.ds(start + (chip ^ m) * units, units)] = pieces[c * chips + m][...]
+            if c > 0:
+                table[pl.ds(start + m * units, units)] = whole_ref[m]
+            else:
+                table[pl.ds(start + (chip ^ m) * units, units)] = pieces[m][...]
         order += [(r, start + i * bands, len(rows) * bands) for i, r in enumerate(rows)]
         start += units * chips
 
-    turn = shelf_ref[Shelf(chunks[1], height, blocks, dates).back]
+    fetch_turn.wait()
+    turn = turn_held[:, turn_cols]
 
     def store(step, b):
         here = pl.ds(step * SUB * height, SUB * height)
@@ -395,7 +412,8 @@
     for step in range(dates // SUB):
         at = pl.ds(step * SUB, SUB)
         here = pl.ds(step * SUB * height, SUB * height)
-        cover = shelf_ref[here, :].astype(jnp.float32)
+        fetch(step).wait()
+        cover = held[bands, here, :].astype(jnp.float32)
         for b in range(bands):
             seasonal = jnp.concatenate(
                 [
@@ -404,7 +422,7 @@
                 ],
                 axis=0,
             )
-            made[b, here, :] = masked_ref[b, here, :].astype(jnp.float32) - cover * product(turn, seasonal)
+            made[b, here, :] = held[b, here, :].astype(jnp.float32) - cover * product(turn, seasonal)
             store(step, b).start()
     for step in range(dates // SUB):
         for b in range(bands):
@@ -417,17 +435,19 @@
     lines = dates * height
     return pl.pallas_call(
         functools.partial(anomaly_kernel, chunks, chips),
-        in_specs=[pl.BlockSpec(memory_space=pltpu.VMEM)] * (1 + len(pieces)),
+        in_specs=[pl.BlockSpec(memory_space=pltpu.HBM)] + [pl.BlockSpec(memory_space=pltpu.VMEM)] * len(pieces),
         out_specs=pl.BlockSpec(memory_space=pl.ANY),
         out_shape=jax.ShapeDtypeStruct((bands, lines, cols), jnp.float32),
         scratch_shapes=[
             pltpu.VMEM((bands * cols // LANES * height, dates, LANES), jnp.bfloat16),
+            pltpu.VMEM((bands + 1, lines, cols), jnp.bfloat16),
+            pltpu.VMEM((SUB * height, cols), jnp.bfloat16),
             pltpu.VMEM((bands, lines, cols), jnp.float32),
-            pltpu.SemaphoreType.DMA((dates // SUB, bands)),
+            pltpu.SemaphoreType.DMA((dates // SUB, bands + 2)),
         ],
-        compiler_params=pltpu.CompilerParams(vmem_limit_bytes=16 * MIB),
+        compiler_params=pltpu.CompilerParams(vmem_limit_bytes=20 * MIB),
         name="anomaly",
-    )(masked, *pieces)
+    )(pltpu.with_memory_space_constraint(masked, pltpu.HBM), *pieces)
 
 
 def exchange(pieces, peers):
@@ -454,13 +474,15 @@
     edges = smooth_rest(masked, height, (before, after), chunks[1], chips)
     outer = exchange(edges, peers)
     high, low = filter_matrix(harmonics, dates, peers)
-    results, after = [], [high, edges[0]]
-    for pieces in (inner, outer):
-        own = pack(pieces, after)
-        other = lax.ppermute(own, DATE, [(i, i ^ 1) for i in range(peers)])
-        made = apply_filter(high, low, own, other, chips)
-        results += exchange(made, peers)
-        after = [made[0]]
+    own = pack(inner, (high, edges[0]), 1)
+    other = lax.ppermute(own, DATE, [(i, i ^ 1) for i in range(peers)])
+    made = apply_filter(high, low, (own, other), chips)
+    results = exchange(made, peers)
+    own = pack(outer, (made[0],), 2)
+    both = lax.all_to_all(own, DATE, 0, 0, axis_index_groups=[[i, i + 1] for i in range(0, peers, 2)])
+    made = apply_filter(high, low, (both,), chips)
+    cores = [list(range(core, peers, 2)) for core in range(2)]
+    results.append(lax.all_to_all(made, DATE, 0, 0, axis_index_groups=cores))
     return anomaly(masked, height, chunks, results, chips).reshape(reflectance.shape)
 
 

time: 65.4 us -> 64 us (0.979)
  waiting for transfers between devices: 29.1 us -> 21.8 us
  blocking collectives: 0 us -> 4.58 us
  Pallas kernels: 13.8 us -> 15.8 us
  starting transfers between devices: 21.2 us -> 20.4 us
    ppermute x12 -> x9, waiting for transfers between devices: 22.3 us -> 10.4 us  [exchange(): lax.ppermute(pieces[m], DATE, [(i, i ^ 2 * m) for i in range(peers)])]
    all_to_all x0 -> x1, blocking collectives: none -> 4.58 us  [on_device(): lax.all_to_all(own, DATE, 0, 0, axis_index_groups=[[i, i + 1] for i in ra...]
    all_to_all x0 -> x1, waiting for transfers between devices: none -> 4.53 us  [on_device(): results.append(lax.all_to_all(made, DATE, 0, 0, axis_index_groups=cores))]
    ppermute x12 -> x9, starting transfers between devices: 15.8 us -> 11.7 us  [exchange(): lax.ppermute(pieces[m], DATE, [(i, i ^ 2 * m) for i in range(peers)])]
    all_to_all x0 -> x1, starting transfers between devices: none -> 3.47 us  [on_device(): results.append(lax.all_to_all(made, DATE, 0, 0, axis_index_groups=cores))]
    pallas_call x1, Pallas kernels: 2.47 us -> 3.6 us  [anomaly(): pl.pallas_call(functools.partial(anomaly_kernel, chunks, chips), in_specs...]
    pallas_call x4, Pallas kernels: 5.57 us -> 6.44 us  [the longest x2 5.99 us: apply_filter(): pl.pallas_call(functools.partial(apply_kernel, chips, shared), out_shape=...]
  transfers between devices with their start and end apart: 16 -> 13, of which waited for: 9 -> 6; matrix products, arithmetic and copies ran while one was open for 1% -> 1% of each run, Pallas kernels for 10% -> 12%
where the time goes in v1:
time: 64 us; the launch traced here: 63.7 us
  waiting for transfers between devices  21.8 us (34%)
  starting transfers between devices  20.4 us (32%)
  Pallas kernels  15.8 us (25%)
  blocking collectives  4.58 us (7%)
  other arithmetic  0.72 us (1%)
    ppermute x9, starting transfers between devices, exchange(): lax.ppermute(pieces[m], DATE, [(i, i ^ 2 * m) for i in range(peers)])  11.7 us
    ppermute x9, waiting for transfers between devices, exchange(): lax.ppermute(pieces[m], DATE, [(i, i ^ 2 * m) for i in range(peers)])  10.4 us
    pallas_call x2, Pallas kernels, apply_filter(): pl.pallas_call(functools.partial(apply_kernel, chips, shared), out_shape=...  5.99 us
    all_to_all x1, blocking collectives, on_device(): lax.all_to_all(own, DATE, 0, 0, axis_index_groups=[[i, i + 1] for i in ra...  4.58 us
    all_to_all x1, waiting for transfers between devices, on_device(): results.append(lax.all_to_all(made, DATE, 0, 0, axis_index_groups=cores))  4.53 us
    pallas_call x1, Pallas kernels, smooth_first(): pl.pallas_call(functools.partial(first_kernel, chunks, chips), in_specs=[...  4.4 us
    ppermute x1, waiting for transfers between devices, on_device(): after = lax.ppermute(first, TILE, [(j, i) for i, j in up])  4.13 us
    ppermute x1, starting transfers between devices, on_device(): before = lax.ppermute(last, TILE, up)  3.95 us
  transfers between devices with their start and end apart: 13, of which 6 were waited for; matrix products, arithmetic and copies ran while one was open for 1% of the time, Pallas kernels for 12%

profile of v1, /device:TPU:0, one launch (start us, length us, event | category | flops | bytes accessed | tf_op | source)
XLA Modules:
  0.0 63.7 jit_solution(10873993610590373556)
XLA Ops:
  0.0 4.4 %smooth_first.1 = (bf16[12,128,128]{2,1,0:T(8,128)(2,1)S(1)}, bf16[12,128,128]{2,1,0:T(8,128)(2,1)S(1)}, bf16[12,128,128]{2,1,0:T(8,128)(2,1)S(1)}, bf16[12,128,...) custom-call(bf16[2,1024,512]{2,1,0:T(8,128)(2,1)} %bitcast.3, ...), custom_call_target="tpu_custom_call" | custom-call | tf_op jit(solution)/shard_map/smooth_first/pallas_call | solution.py:196
  4.4 3.0 %collective-permute-start = (bf16[12,128,128]{2,1,0:T(8,128)(2,1)S(1)}, bf16[12,128,128]{2,1,0:T(8,128)(2,1)S(1)}, u32[]{:S(2)}, u32[]{:S(2)}) collective-permute-start(bf16[12,128,128]{2,1,0:T(8,128)(2,1)S(1)} %get-tuple-element.28), channel_id=1, source_target_pairs={{0,8},{4,12},{8,0},{12,4},{16,24},{20,28},{24,16},{28,20},{1,9},{5... | collective-permute-start | bytes 1179656 | tf_op jit(solution)/shard_map/ppermute | solution.py:456
  7.4 1.5 %collective-permute-start.1 = (bf16[12,128,128]{2,1,0:T(8,128)(2,1)S(1)}, bf16[12,128,128]{2,1,0:T(8,128)(2,1)S(1)}, u32[]{:S(2)}, u32[]{:S(2)}) collective-permute-start(bf16[12,128,128]{2,1,0:T(8,128)(2,1)S(1)} %get-tuple-element.29), channel_id=1, source_target_pairs={{0,16},{4,20},{8,24},{12,28},{16,0},{20,4},{24,8},{28,12},{1,17},{... | collective-permute-start | bytes 1179656 | tf_op jit(solution)/shard_map/ppermute | solution.py:456
  9.0 4.0 %collective-permute-start.3 = (bf16[9,128,128]{2,1,0:T(8,128)(2,1)S(1)}, bf16[9,128,128]{2,1,0:T(8,128)(2,1)S(1)}, u32[]{:S(2)}, u32[]{:S(2)}) collective-permute-start(bf16[9,128,128]{2,1,0:T(8,128)(2,1)S(1)} %get-tuple-element.33), channel_id=1, source_target_pairs={{0,1},{1,2},{2,3},{4,5},{5,6},{6,7},{8,9},{9,10},{10,11},{12,13},{... | collective-permute-start | bytes 884744 | tf_op jit(solution)/shard_map/ppermute | solution.py:472
  13.0 1.3 %collective-permute-start.4 = (bf16[9,128,128]{2,1,0:T(8,128)(2,1)S(1)}, bf16[9,128,128]{2,1,0:T(8,128)(2,1)S(1)}, u32[]{:S(2)}, u32[]{:S(2)}) collective-permute-start(bf16[9,128,128]{2,1,0:T(8,128)(2,1)S(1)} %get-tuple-element.34), channel_id=1, source_target_pairs={{1,0},{2,1},{3,2},{5,4},{6,5},{7,6},{9,8},{10,9},{11,10},{13,12},{... | collective-permute-start | bytes 884744 | tf_op jit(solution)/shard_map/ppermute | solution.py:473
  14.3 0.6 fusion.9
  15.6 2.7 %collective-permute-done.3.before_ref = bf16[9,128,128]{2,1,0:T(8,128)(2,1)S(1)} collective-permute-done((bf16[9,128,128]{2,1,0:T(8,128)(2,1)S(1)}, bf16[9,128,128]{2,1,0:T(8,128)(2,1)S(1)}, u32[]{:S(2)}, u32[]{:S(2)}) %collective-permute-start.3) | collective-permute-done | bytes 294944 | tf_op jit(solution)/shard_map/ppermute | solution.py:472
  18.4 4.1 %collective-permute-done.4.after_ref = bf16[9,128,128]{2,1,0:T(8,128)(2,1)S(1)} collective-permute-done((bf16[9,128,128]{2,1,0:T(8,128)(2,1)S(1)}, bf16[9,128,128]{2,1,0:T(8,128)(2,1)S(1)}, u32[]{:S(2)}, u32[]{:S(2)}) %collective-permute-start.4) | collective-permute-done | bytes 294944 | tf_op jit(solution)/shard_map/ppermute | solution.py:473
  22.5 1.0 %smooth_rest.1 = (bf16[4,128,128]{2,1,0:T(8,128)(2,1)S(1)}, bf16[4,128,128]{2,1,0:T(8,128)(2,1)S(1)}, bf16[4,128,128]{2,1,0:T(8,128)(2,1)S(1)}, bf16[4,128,128]{2,1,0:T(8,128)(2,1)S(1)}) custom-call(bf16[3,1472,512]{2,1,0:T(8,128)(2,1)S(1)} %get-tuple-element.24.masked_ref, bf16[9,128,128]{2,1,0:T(8,128)(2,1)S(1)} %collective-permute-done.3.before_ref, ...), custom_call_target="tpu_custom_call" | custom-call | tf_op jit(solution)/shard_map/smooth_rest/pallas_call | solution.py:259
  23.5 2.9 %collective-permute-done.1.refs_2_ = bf16[12,128,128]{2,1,0:T(8,128)(2,1)S(1)} collective-permute-done((bf16[12,128,128]{2,1,0:T(8,128)(2,1)S(1)}, bf16[12,128,128]{2,1,0:T(8,128)(2,1)S(1)}, u32[]{:S(2)}, u32[]{:S(2)}) %collective-permute-start.1) | collective-permute-done | bytes 393248 | tf_op jit(solution)/shard_map/ppermute | solution.py:456
  26.8 1.3 %collective-permute-start.9 = (bf16[4,128,128]{2,1,0:T(8,128)(2,1)S(1)}, bf16[4,128,128]{2,1,0:T(8,128)(2,1)S(1)}, u32[]{:S(2)}, u32[]{:S(2)}) collective-permute-start(bf16[4,128,128]{2,1,0:T(8,128)(2,1)S(1)} %get-tuple-element.40), channel_id=1, source_target_pairs={{0,8},{4,12},{8,0},{12,4},{16,24},{20,28},{24,16},{28,20},{1,9},{5... | collective-permute-start | bytes 393224 | tf_op jit(solution)/shard_map/ppermute | solution.py:456
  28.1 0.8 %collective-permute-start.10 = (bf16[4,128,128]{2,1,0:T(8,128)(2,1)S(1)}, bf16[4,128,128]{2,1,0:T(8,128)(2,1)S(1)}, u32[]{:S(2)}, u32[]{:S(2)}) collective-permute-start(bf16[4,128,128]{2,1,0:T(8,128)(2,1)S(1)} %get-tuple-element.41), channel_id=1, source_target_pairs={{0,16},{4,20},{8,24},{12,28},{16,0},{20,4},{24,8},{28,12},{1,17},{... | collective-permute-start | bytes 393224 | tf_op jit(solution)/shard_map/ppermute | solution.py:456
  28.9 1.4 %collective-permute-start.11 = (bf16[4,128,128]{2,1,0:T(8,128)(2,1)S(1)}, bf16[4,128,128]{2,1,0:T(8,128)(2,1)S(1)}, u32[]{:S(2)}, u32[]{:S(2)}) collective-permute-start(bf16[4,128,128]{2,1,0:T(8,128)(2,1)S(1)} %get-tuple-element.42), channel_id=1, source_target_pairs={{0,24},{4,28},{8,16},{12,20},{16,8},{20,12},{24,0},{28,4},{1,25},{... | collective-permute-start | bytes 393224 | tf_op jit(solution)/shard_map/ppermute | solution.py:456
  30.4 3.7 %apply_filter.2 = (bf16[12,128,128]{2,1,0:T(8,128)(2,1)S(1)}, bf16[12,128,128]{2,1,0:T(8,128)(2,1)S(1)}, bf16[12,128,128]{2,1,0:T(8,128)(2,1)S(1)}, bf16[12,128,128]{2,1,0:T(8,128)(2,1)S(1)}) custom-call(bf16[512,1024]{1,0:T(8,128)(2,1)S(1)} %get-tuple-element.25.refs_4_.high_ref, bf16[512,1024]{1,0:T(8,128)(2,1)S(1)} %get-tuple-element.26.low_ref, ...), custom_call_target="tpu_custom_call" | custom-call | tf_op jit(solution)/shard_map/apply_filter/pallas_call | solution.py:368
  34.1 1.3 %collective-permute-start.6 = (bf16[12,128,128]{2,1,0:T(8,128)(2,1)S(1)}, bf16[12,128,128]{2,1,0:T(8,128)(2,1)S(1)}, u32[]{:S(2)}, u32[]{:S(2)}) collective-permute-start(bf16[12,128,128]{2,1,0:T(8,128)(2,1)S(1)} %get-tuple-element.37), channel_id=1, source_target_pairs={{0,8},{4,12},{8,0},{12,4},{16,24},{20,28},{24,16},{28,20},{1,9},{5... | collective-permute-start | bytes 1179656 | tf_op jit(solution)/shard_map/ppermute | solution.py:456
  35.4 0.8 %collective-permute-start.7 = (bf16[12,128,128]{2,1,0:T(8,128)(2,1)S(1)}, bf16[12,128,128]{2,1,0:T(8,128)(2,1)S(1)}, u32[]{:S(2)}, u32[]{:S(2)}) collective-permute-start(bf16[12,128,128]{2,1,0:T(8,128)(2,1)S(1)} %get-tuple-element.38), channel_id=1, source_target_pairs={{0,16},{4,20},{8,24},{12,28},{16,0},{20,4},{24,8},{28,12},{1,17},{... | collective-permute-start | bytes 1179656 | tf_op jit(solution)/shard_map/ppermute | solution.py:456
  36.2 1.4 %collective-permute-start.8 = (bf16[12,128,128]{2,1,0:T(8,128)(2,1)S(1)}, bf16[12,128,128]{2,1,0:T(8,128)(2,1)S(1)}, u32[]{:S(2)}, u32[]{:S(2)}) collective-permute-start(bf16[12,128,128]{2,1,0:T(8,128)(2,1)S(1)} %get-tuple-element.39), channel_id=1, source_target_pairs={{0,24},{4,28},{8,16},{12,20},{16,8},{20,12},{24,0},{28,4},{1,25},{... | collective-permute-start | bytes 1179656 | tf_op jit(solution)/shard_map/ppermute | solution.py:456
  37.8 4.6 %all_to_all.10.refs_0_ = bf16[2,512,512]{2,1,0:T(8,128)(2,1)S(1)} all-to-all(bf16[2,512,512]{2,1,0:T(8,128)(2,1)S(1)} %pack.3), channel_id=1, replica_groups={{0,4},{8,12},{16,20},{24,28},{1,5},{9,13},{17,21},{25,29},{2,6},{10,14}..., dimensions={0} | all-to-all | bytes 2097152 | tf_op jit(solution)/shard_map/all_to_all | solution.py:482
  42.4 2.3 %apply_filter.3 = bf16[4,4,128,128]{3,2,1,0:T(8,128)(2,1)} custom-call(bf16[512,1024]{1,0:T(8,128)(2,1)S(1)} %get-tuple-element.25.refs_4_.high_ref, bf16[512,1024]{1,0:T(8,128)(2,1)S(1)} %get-tuple-element.26.low_ref, bf16[2,512,512]{2,1,0:T(8,128)(2,1)S(1)} %all_to_all.10.refs_0_), custom_call_target="tpu_custom_call" | custom-call | tf_op jit(solution)/shard_map/apply_filter/pallas_call | solution.py:368
  44.7 3.5 %all-to-all-start.1 = ((bf16[4,4,128,128]{3,2,1,0:T(8,128)(2,1)}), bf16[4,4,128,128]{3,2,1,0:T(8,128)(2,1)S(1)}, u32[]{:S(2)}, u32[]{:S(2)}) async-start(bf16[4,4,128,128]{3,2,1,0:T(8,128)(2,1)} %apply_filter.3), calls=%async_computation.1 | async-start | bytes 1048576 | tf_op jit(solution)/shard_map/all_to_all | solution.py:485
  48.2 6.6 %collective-permute-done.7.refs_2_ = bf16[12,128,128]{2,1,0:T(8,128)(2,1)S(1)} collective-permute-done((bf16[12,128,128]{2,1,0:T(8,128)(2,1)S(1)}, bf16[12,128,128]{2,1,0:T(8,128)(2,1)S(1)}, u32[]{:S(2)}, u32[]{:S(2)}) %collective-permute-start.7) | collective-permute-done | bytes 393248 | tf_op jit(solution)/shard_map/ppermute | solution.py:456
  54.8 0.8 %collective-permute-done.8.refs_3_ = bf16[12,128,128]{2,1,0:T(8,128)(2,1)S(1)} collective-permute-done((bf16[12,128,128]{2,1,0:T(8,128)(2,1)S(1)}, bf16[12,128,128]{2,1,0:T(8,128)(2,1)S(1)}, u32[]{:S(2)}, u32[]{:S(2)}) %collective-permute-start.8) | collective-permute-done | bytes 393248 | tf_op jit(solution)/shard_map/ppermute | solution.py:456
  55.6 4.5 %all-to-all-done.1.refs_4_ = bf16[4,4,128,128]{3,2,1,0:T(8,128)(2,1)S(1)} async-done(((bf16[4,4,128,128]{3,2,1,0:T(8,128)(2,1)}), bf16[4,4,128,128]{3,2,1,0:T(8,128)(2,1)S(1)}, u32[]{:S(2)}, u32[]{:S(2)}) %all-to-all-start.1) | async-done | bytes 524320 | tf_op jit(solution)/shard_map/all_to_all | solution.py:485
  60.1 3.6 %anomaly.1 = f32[2,1024,512]{2,1,0:T(8,128)} custom-call(bf16[3,1472,512]{2,1,0:T(8,128)(2,1)} %copy-done, bf16[12,128,128]{2,1,0:T(8,128)(2,1)S(1)} %get-tuple-element.36.refs_4_.refs_0_, bf16[12,128,128]{2,1,0:T(8,128)(2,1)S(1)} %collective-permute-done.6.refs_1_, bf16[12,128,128]{2,1,0:T(8,128)(2,1)S(1)} %collective-permute-done.7.refs_2_, ...), custom_call_target="tpu_custom_call" | custom-call | tf_op jit(solution)/shard_map/anomaly/pallas_call | solution.py:436
  (20 shorter events, 1.3 us)
Async XLA Ops:
  0.0 14.3 %copy-start.1 = (s32[256]{0:T(256)S(1)}, s32[256]{0:T(256)}, u32[]{:S(2)}) copy-start(s32[256]{0:T(256)} %param.5) | copy-start | bytes 3076
  4.4 19.1 %copy-start = (bf16[3,1472,512]{2,1,0:T(8,128)(2,1)}, bf16[3,1472,512]{2,1,0:T(8,128)(2,1)S(1)}, u32[]{:S(2)}) copy-start(bf16[3,1472,512]{2,1,0:T(8,128)(2,1)S(1)} %get-tuple-element.24.masked_ref) | copy-start | bytes 13565956
  4.4 19.1 %collective-permute-start = (bf16[12,128,128]{2,1,0:T(8,128)(2,1)S(1)}, bf16[12,128,128]{2,1,0:T(8,128)(2,1)S(1)}, u32[]{:S(2)}, u32[]{:S(2)}) collective-permute-start(bf16[12,128,128]{2,1,0:T(8,128)(2,1)S(1)} %get-tuple-element.28), channel_id=1, source_target_pairs={{0,8},{4,12},{8,0},{12,4},{16,24},{20,28},{24,16},{28,20},{1,9},{5... | collective-permute-start | bytes 1179656 | tf_op jit(solution)/shard_map/ppermute | solution.py:456
  7.4 19.0 %collective-permute-start.1 = (bf16[12,128,128]{2,1,0:T(8,128)(2,1)S(1)}, bf16[12,128,128]{2,1,0:T(8,128)(2,1)S(1)}, u32[]{:S(2)}, u32[]{:S(2)}) collective-permute-start(bf16[12,128,128]{2,1,0:T(8,128)(2,1)S(1)} %get-tuple-element.29), channel_id=1, source_target_pairs={{0,16},{4,20},{8,24},{12,28},{16,0},{20,4},{24,8},{28,12},{1,17},{... | collective-permute-start | bytes 1179656 | tf_op jit(solution)/shard_map/ppermute | solution.py:456
  8.9 17.5 %collective-permute-start.2 = (bf16[12,128,128]{2,1,0:T(8,128)(2,1)S(1)}, bf16[12,128,128]{2,1,0:T(8,128)(2,1)S(1)}, u32[]{:S(2)}, u32[]{:S(2)}) collective-permute-start(bf16[12,128,128]{2,1,0:T(8,128)(2,1)S(1)} %get-tuple-element.30), channel_id=1, source_target_pairs={{0,24},{4,28},{8,16},{12,20},{16,8},{20,12},{24,0},{28,4},{1,25},{... | collective-permute-start | bytes 1179656 | tf_op jit(solution)/shard_map/ppermute | solution.py:456
  9.0 9.4 %collective-permute-start.3 = (bf16[9,128,128]{2,1,0:T(8,128)(2,1)S(1)}, bf16[9,128,128]{2,1,0:T(8,128)(2,1)S(1)}, u32[]{:S(2)}, u32[]{:S(2)}) collective-permute-start(bf16[9,128,128]{2,1,0:T(8,128)(2,1)S(1)} %get-tuple-element.33), channel_id=1, source_target_pairs={{0,1},{1,2},{2,3},{4,5},{5,6},{6,7},{8,9},{9,10},{10,11},{12,13},{... | collective-permute-start | bytes 884744 | tf_op jit(solution)/shard_map/ppermute | solution.py:472
  13.0 9.5 %collective-permute-start.4 = (bf16[9,128,128]{2,1,0:T(8,128)(2,1)S(1)}, bf16[9,128,128]{2,1,0:T(8,128)(2,1)S(1)}, u32[]{:S(2)}, u32[]{:S(2)}) collective-permute-start(bf16[9,128,128]{2,1,0:T(8,128)(2,1)S(1)} %get-tuple-element.34), channel_id=1, source_target_pairs={{1,0},{2,1},{3,2},{5,4},{6,5},{7,6},{9,8},{10,9},{11,10},{13,12},{... | collective-permute-start | bytes 884744 | tf_op jit(solution)/shard_map/ppermute | solution.py:473
  26.7 3.6 %collective-permute-start.5 = (bf16[512,1536]{1,0:T(8,128)(2,1)S(1)}, bf16[512,1536]{1,0:T(8,128)(2,1)S(1)}, u32[]{:S(2)}, u32[]{:S(2)}) collective-permute-start(bf16[512,1536]{1,0:T(8,128)(2,1)S(1)} %pack.2.refs_0_), channel_id=1, source_target_pairs={{0,4},{4,0},{8,12},{12,8},{16,20},{20,16},{24,28},{28,24},{1,5},{5... | collective-permute-start | bytes 4718600 | tf_op jit(solution)/shard_map/ppermute | solution.py:478
  26.8 9.4 %collective-permute-start.9 = (bf16[4,128,128]{2,1,0:T(8,128)(2,1)S(1)}, bf16[4,128,128]{2,1,0:T(8,128)(2,1)S(1)}, u32[]{:S(2)}, u32[]{:S(2)}) collective-permute-start(bf16[4,128,128]{2,1,0:T(8,128)(2,1)S(1)} %get-tuple-element.40), channel_id=1, source_target_pairs={{0,8},{4,12},{8,0},{12,4},{16,24},{20,28},{24,16},{28,20},{1,9},{5... | collective-permute-start | bytes 393224 | tf_op jit(solution)/shard_map/ppermute | solution.py:456
  28.1 9.6 %collective-permute-start.10 = (bf16[4,128,128]{2,1,0:T(8,128)(2,1)S(1)}, bf16[4,128,128]{2,1,0:T(8,128)(2,1)S(1)}, u32[]{:S(2)}, u32[]{:S(2)}) collective-permute-start(bf16[4,128,128]{2,1,0:T(8,128)(2,1)S(1)} %get-tuple-element.41), channel_id=1, source_target_pairs={{0,16},{4,20},{8,24},{12,28},{16,0},{20,4},{24,8},{28,12},{1,17},{... | collective-permute-start | bytes 393224 | tf_op jit(solution)/shard_map/ppermute | solution.py:456
  28.9 8.7 %collective-permute-start.11 = (bf16[4,128,128]{2,1,0:T(8,128)(2,1)S(1)}, bf16[4,128,128]{2,1,0:T(8,128)(2,1)S(1)}, u32[]{:S(2)}, u32[]{:S(2)}) collective-permute-start(bf16[4,128,128]{2,1,0:T(8,128)(2,1)S(1)} %get-tuple-element.42), channel_id=1, source_target_pairs={{0,24},{4,28},{8,16},{12,20},{16,8},{20,12},{24,0},{28,4},{1,25},{... | collective-permute-start | bytes 393224 | tf_op jit(solution)/shard_map/ppermute | solution.py:456
  34.1 14.1 %collective-permute-start.6 = (bf16[12,128,128]{2,1,0:T(8,128)(2,1)S(1)}, bf16[12,128,128]{2,1,0:T(8,128)(2,1)S(1)}, u32[]{:S(2)}, u32[]{:S(2)}) collective-permute-start(bf16[12,128,128]{2,1,0:T(8,128)(2,1)S(1)} %get-tuple-element.37), channel_id=1, source_target_pairs={{0,8},{4,12},{8,0},{12,4},{16,24},{20,28},{24,16},{28,20},{1,9},{5... | collective-permute-start | bytes 1179656 | tf_op jit(solution)/shard_map/ppermute | solution.py:456
  35.4 19.4 %collective-permute-start.7 = (bf16[12,128,128]{2,1,0:T(8,128)(2,1)S(1)}, bf16[12,128,128]{2,1,0:T(8,128)(2,1)S(1)}, u32[]{:S(2)}, u32[]{:S(2)}) collective-permute-start(bf16[12,128,128]{2,1,0:T(8,128)(2,1)S(1)} %get-tuple-element.38), channel_id=1, source_target_pairs={{0,16},{4,20},{8,24},{12,28},{16,0},{20,4},{24,8},{28,12},{1,17},{... | collective-permute-start | bytes 1179656 | tf_op jit(solution)/shard_map/ppermute | solution.py:456
  36.2 19.4 %collective-permute-start.8 = (bf16[12,128,128]{2,1,0:T(8,128)(2,1)S(1)}, bf16[12,128,128]{2,1,0:T(8,128)(2,1)S(1)}, u32[]{:S(2)}, u32[]{:S(2)}) collective-permute-start(bf16[12,128,128]{2,1,0:T(8,128)(2,1)S(1)} %get-tuple-element.39), channel_id=1, source_target_pairs={{0,24},{4,28},{8,16},{12,20},{16,8},{20,12},{24,0},{28,4},{1,25},{... | collective-permute-start | bytes 1179656 | tf_op jit(solution)/shard_map/ppermute | solution.py:456
  44.7 15.5 %all-to-all-start.1 = ((bf16[4,4,128,128]{3,2,1,0:T(8,128)(2,1)}), bf16[4,4,128,128]{3,2,1,0:T(8,128)(2,1)S(1)}, u32[]{:S(2)}, u32[]{:S(2)}) async-start(bf16[4,4,128,128]{3,2,1,0:T(8,128)(2,1)} %apply_filter.3), calls=%async_computation.1 | async-start | bytes 1048576 | tf_op jit(solution)/shard_map/all_to_all | solution.py:485

commit v2 on v1

--- a/solution.py
+++ b/solution.py
@@ -11,7 +11,19 @@
 LANES = 128
 SUB = 32
 MIB = 2**20
+CLOUD = 1e30
 DATE, TILE = ("date", "tile")
+
+
+def apart(m, chips, core):
+    bits = (chips - m) % chips
+    width = chips.bit_length() - 1
+    return sum((bits >> k & 1) << (width - 1 - k) for k in range(width)) if core else bits
+
+
+def partner(m, chips):
+    me = lax.axis_index(DATE)
+    return (me // 2) ^ jnp.where(me % 2 == 0, apart(m, chips, 0), apart(m, chips, 1))
 
 
 def padded(size):
@@ -96,8 +108,7 @@
         start += width
         self.near = [(pl.ds(start + step * lines, lines), pl.ds(0, width)) for step in range(dates // SUB)]
         self.turn = (pl.ds(start, lines), pl.ds(width, SUB * height))
-        self.back = (pl.ds(start + lines, SUB * height), pl.ds(width, SUB * height))
-        self.size = start + max(dates // SUB * lines, lines + SUB * height)
+        self.size = start + dates // SUB * lines
 
 
 def smooth_lines(down, scale, lane):
@@ -117,9 +128,8 @@
 
 def give_pieces(table, pieces):
     units = table.shape[0] // len(pieces)
-    chip = lax.axis_index(DATE) // 2
     for m, piece in enumerate(pieces):
-        piece[...] = table[pl.ds((chip ^ m) * units, units)]
+        piece[...] = table[pl.ds(partner(m, len(pieces)) * units, units)]
 
 
 def first_kernel(chunks, chips, refl_ref, clear_ref, *refs):
@@ -154,7 +164,6 @@
     turn_rest = turn_matrix(rest, height)
     shelf_ref[shelf.box] = box
     shelf_ref[shelf.turn] = turn_rest
-    shelf_ref[shelf.back] = back_matrix(rows + rest, height)
     lane = lax.broadcasted_iota(jnp.int32, (len(rows) * SUB, cols), 1)
     fetch_clear.wait()
     turn_flags(clear_held, flags_in, flags)
@@ -172,10 +181,11 @@
         shelf_ref[shelf.near[step]] = product(turn_rest, lines).astype(jnp.bfloat16)
         count = product(product(turn, lines).astype(jnp.bfloat16), box)
         scale = 1.0 / jnp.maximum(count, 1.0)
+        cloud = CLOUD - CLOUD * cover
         fetch(step).wait()
         for b in range(bands):
             masked = held_ref[b, here, :] * cover
-            masked_ref[b, here, :] = masked
+            masked_ref[b, here, :] = masked + cloud
             ends = product(edges, masked).astype(jnp.bfloat16)
             for i, ref in enumerate((first_ref, last_ref)):
                 for k in range(blocks):
@@ -230,7 +240,7 @@
             count = add_row(count, place, product(ref[flat, at, :], box))
         scale = 1.0 / jnp.maximum(count, 1.0)
         for b in range(bands):
-            down = product(turn, masked_ref[b, here, :])
+            down = product(turn, masked_ref[b, here, :] * shelf_ref[here, :])
             for place, ref in halo:
                 extra = jnp.concatenate([ref[b * blocks + k, at, :] for k in range(blocks)], axis=1)
                 down = add_row(down, place, extra.astype(jnp.float32))
@@ -316,7 +326,7 @@
     units, dates, lanes = pieces[0].shape
     chip = lax.axis_index(DATE) // 2
     for m in range(chips):
-        at = pl.multiple_of((chip ^ m) * dates, dates)
+        at = pl.multiple_of(partner(m, chips) * dates, dates)
         for i in range(units):
             part = (pl.ds(at, dates), pl.ds(i * lanes, lanes))
             for side in ((0,), (1,)) if len(out_ref.shape) == 3 else ((),):
@@ -355,7 +365,7 @@
         result[at, :] = total
 
     for m in range(chips):
-        at = m * dates if shared else pl.multiple_of((chip ^ m) * dates, dates)
+        at = m * dates if shared else pl.multiple_of(partner(m, chips) * dates, dates)
         out = outs.at[m] if shared else outs[m]
         for i in range(units):
             out[i] = result[pl.ds(at, dates), i * lanes : (i + 1) * lanes].astype(jnp.bfloat16)
@@ -375,22 +385,19 @@
 
 
 def anomaly_kernel(chunks, chips, masked_ref, *refs):
-    pieces, whole_ref, (out_ref, table, held, turn_held, made, sems) = refs[:chips], refs[chips], refs[chips + 1 :]
+    pieces, whole_ref, (out_ref, table, held, made, sems) = refs[:chips], refs[chips], refs[chips + 1 :]
     bands, lines, cols = made.shape
     dates = table.shape[1]
     height = lines // dates
     blocks = cols // LANES
     chip = lax.axis_index(DATE) // 2
-    turn_at, turn_cols = Shelf(chunks[1], height, blocks, dates).back
-    fetch_turn = pltpu.make_async_copy(masked_ref.at[bands, turn_at], turn_held, sems.at[0, bands + 1])
-
     def fetch(step):
         here = pl.ds(step * SUB * height, SUB * height)
-        return pltpu.make_async_copy(masked_ref.at[:, here], held.at[:, here], sems.at[step, bands])
-
-    fetch_turn.start()
+        return pltpu.make_async_copy(masked_ref.at[0:bands, here], held.at[:, here], sems.at[step, bands])
+
     for step in range(dates // SUB):
         fetch(step).start()
+    turn = back_matrix(chunks[0] + chunks[1], height)
     order, start = [], 0
     for c, rows in enumerate(chunks):
         units = whole_ref.shape[1] if c > 0 else pieces[0].shape[0]
@@ -398,12 +405,9 @@
             if c > 0:
                 table[pl.ds(start + m * units, units)] = whole_ref[m]
             else:
-                table[pl.ds(start + (chip ^ m) * units, units)] = pieces[m][...]
-        order += [(r, start + i * bands, len(rows) * bands) for i, r in enumerate(rows)]
+                table[pl.ds(start + partner(m, chips) * units, units)] = pieces[m][...]
+        order += [(start + i * bands, len(rows) * bands) for i in range(len(rows))]
         start += units * chips
-
-    fetch_turn.wait()
-    turn = turn_held[:, turn_cols]
 
     def store(step, b):
         here = pl.ds(step * SUB * height, SUB * height)
@@ -413,16 +417,16 @@
         at = pl.ds(step * SUB, SUB)
         here = pl.ds(step * SUB * height, SUB * height)
         fetch(step).wait()
-        cover = held[bands, here, :].astype(jnp.float32)
         for b in range(bands):
             seasonal = jnp.concatenate(
                 [
                     jnp.concatenate([table[first + k * step_k + b, at, :] for k in range(blocks)], axis=1)
-                    for _, first, step_k in order
+                    for first, step_k in order
                 ],
                 axis=0,
             )
-            made[b, here, :] = held[b, here, :].astype(jnp.float32) - cover * product(turn, seasonal)
+            clear = held[b, here, :].astype(jnp.float32)
+            made[b, here, :] = jnp.where(clear < CLOUD / 2, clear - product(turn, seasonal), 0.0)
             store(step, b).start()
     for step in range(dates // SUB):
         for b in range(bands):
@@ -440,10 +444,9 @@
         out_shape=jax.ShapeDtypeStruct((bands, lines, cols), jnp.float32),
         scratch_shapes=[
             pltpu.VMEM((bands * cols // LANES * height, dates, LANES), jnp.bfloat16),
-            pltpu.VMEM((bands + 1, lines, cols), jnp.bfloat16),
-            pltpu.VMEM((SUB * height, cols), jnp.bfloat16),
+            pltpu.VMEM((bands, lines, cols), jnp.bfloat16),
             pltpu.VMEM((bands, lines, cols), jnp.float32),
-            pltpu.SemaphoreType.DMA((dates // SUB, bands + 2)),
+            pltpu.SemaphoreType.DMA((dates // SUB, bands + 1)),
         ],
         compiler_params=pltpu.CompilerParams(vmem_limit_bytes=20 * MIB),
         name="anomaly",
@@ -453,7 +456,8 @@
 def exchange(pieces, peers):
     out = list(pieces)
     for m in range(len(pieces) - 1, 0, -1):
-        out[m] = lax.ppermute(pieces[m], DATE, [(i, i ^ (2 * m)) for i in range(peers)])
+        to = [(i, i ^ (2 * apart(m, len(pieces), i % 2))) for i in range(peers)]
+        out[m] = lax.ppermute(pieces[m], DATE, to)
     return out
 
 

time: 64 us -> 63.7 us (level)
  transfers between devices with their start and end apart: 13 -> 13, of which waited for: 6 -> 6; matrix products, arithmetic and copies ran while one was open for 1% -> 2% of each run, Pallas kernels for 12% -> 12%
where the time goes in v2:
time: 63.7 us; the launch traced here: 63.4 us
  waiting for transfers between devices  21.4 us (34%)
  starting transfers between devices  20.6 us (32%)
  Pallas kernels  15.8 us (25%)
  blocking collectives  4.58 us (7%)
  other arithmetic  0.72 us (1%)
    ppermute x9, starting transfers between devices, exchange(): out[m] = lax.ppermute(pieces[m], DATE, to)  11.7 us
    ppermute x9, waiting for transfers between devices, exchange(): out[m] = lax.ppermute(pieces[m], DATE, to)  9.97 us
    pallas_call x2, Pallas kernels, apply_filter(): pl.pallas_call(functools.partial(apply_kernel, chips, shared), out_shape=...  6 us
    all_to_all x1, blocking collectives, on_device(): lax.all_to_all(own, DATE, 0, 0, axis_index_groups=[[i, i + 1] for i in ra...  4.58 us
    all_to_all x1, waiting for transfers between devices, on_device(): results.append(lax.all_to_all(made, DATE, 0, 0, axis_index_groups=cores))  4.53 us
    pallas_call x1, Pallas kernels, smooth_first(): pl.pallas_call(functools.partial(first_kernel, chunks, chips), in_specs=[...  4.51 us
    ppermute x1, waiting for transfers between devices, on_device(): after = lax.ppermute(first, TILE, [(j, i) for i, j in up])  4.13 us
    ppermute x1, starting transfers between devices, on_device(): before = lax.ppermute(last, TILE, up)  3.89 us
  transfers between devices with their start and end apart: 13, of which 6 were waited for; matrix products, arithmetic and copies ran while one was open for 2% of the time, Pallas kernels for 12%

profile of v2, /device:TPU:0, one launch (start us, length us, event | category | flops | bytes accessed | tf_op | source)
XLA Modules:
  0.0 63.4 jit_solution(7674458397647748145)
XLA Ops:
  0.0 4.5 %smooth_first.1 = (bf16[12,128,128]{2,1,0:T(8,128)(2,1)S(1)}, bf16[12,128,128]{2,1,0:T(8,128)(2,1)S(1)}, bf16[12,128,128]{2,1,0:T(8,128)(2,1)S(1)}, bf16[12,128,...) custom-call(bf16[2,1024,512]{2,1,0:T(8,128)(2,1)} %bitcast.3, ...), custom_call_target="tpu_custom_call" | custom-call | tf_op jit(solution)/shard_map/smooth_first/pallas_call | solution.py:206
  4.5 4.0 %collective-permute-start = (bf16[12,128,128]{2,1,0:T(8,128)(2,1)S(1)}, bf16[12,128,128]{2,1,0:T(8,128)(2,1)S(1)}, u32[]{:S(2)}, u32[]{:S(2)}) collective-permute-start(bf16[12,128,128]{2,1,0:T(8,128)(2,1)S(1)} %get-tuple-element.28), channel_id=1, source_target_pairs={{0,24},{4,28},{8,16},{12,20},{16,8},{20,12},{24,0},{28,4},{1,25},{... | collective-permute-start | bytes 1179656 | tf_op jit(solution)/shard_map/ppermute | solution.py:460
  8.5 0.5 collective-permute-start.1
  9.2 3.9 %collective-permute-start.3 = (bf16[9,128,128]{2,1,0:T(8,128)(2,1)S(1)}, bf16[9,128,128]{2,1,0:T(8,128)(2,1)S(1)}, u32[]{:S(2)}, u32[]{:S(2)}) collective-permute-start(bf16[9,128,128]{2,1,0:T(8,128)(2,1)S(1)} %get-tuple-element.33), channel_id=1, source_target_pairs={{0,1},{1,2},{2,3},{4,5},{5,6},{6,7},{8,9},{9,10},{10,11},{12,13},{... | collective-permute-start | bytes 884744 | tf_op jit(solution)/shard_map/ppermute | solution.py:476
  13.1 1.3 %collective-permute-start.4 = (bf16[9,128,128]{2,1,0:T(8,128)(2,1)S(1)}, bf16[9,128,128]{2,1,0:T(8,128)(2,1)S(1)}, u32[]{:S(2)}, u32[]{:S(2)}) collective-permute-start(bf16[9,128,128]{2,1,0:T(8,128)(2,1)S(1)} %get-tuple-element.34), channel_id=1, source_target_pairs={{1,0},{2,1},{3,2},{5,4},{6,5},{7,6},{9,8},{10,9},{11,10},{13,12},{... | collective-permute-start | bytes 884744 | tf_op jit(solution)/shard_map/ppermute | solution.py:477
  14.4 0.6 fusion.9
  15.4 0.4 filter_matrix.1
  15.7 2.7 %collective-permute-done.3.before_ref = bf16[9,128,128]{2,1,0:T(8,128)(2,1)S(1)} collective-permute-done((bf16[9,128,128]{2,1,0:T(8,128)(2,1)S(1)}, bf16[9,128,128]{2,1,0:T(8,128)(2,1)S(1)}, u32[]{:S(2)}, u32[]{:S(2)}) %collective-permute-start.3) | collective-permute-done | bytes 294944 | tf_op jit(solution)/shard_map/ppermute | solution.py:476
  18.5 4.1 %collective-permute-done.4.after_ref = bf16[9,128,128]{2,1,0:T(8,128)(2,1)S(1)} collective-permute-done((bf16[9,128,128]{2,1,0:T(8,128)(2,1)S(1)}, bf16[9,128,128]{2,1,0:T(8,128)(2,1)S(1)}, u32[]{:S(2)}, u32[]{:S(2)}) %collective-permute-start.4) | collective-permute-done | bytes 294944 | tf_op jit(solution)/shard_map/ppermute | solution.py:477
  22.6 1.0 %smooth_rest.1 = (bf16[4,128,128]{2,1,0:T(8,128)(2,1)S(1)}, bf16[4,128,128]{2,1,0:T(8,128)(2,1)S(1)}, bf16[4,128,128]{2,1,0:T(8,128)(2,1)S(1)}, bf16[4,128,128]{2,1,0:T(8,128)(2,1)S(1)}) custom-call(bf16[3,1408,512]{2,1,0:T(8,128)(2,1)S(1)} %get-tuple-element.24.masked_ref, bf16[9,128,128]{2,1,0:T(8,128)(2,1)S(1)} %collective-permute-done.3.before_ref, ...), custom_call_target="tpu_custom_call" | custom-call | tf_op jit(solution)/shard_map/smooth_rest/pallas_call | solution.py:269
  23.6 2.4 %collective-permute-done.1.refs_2_ = bf16[12,128,128]{2,1,0:T(8,128)(2,1)S(1)} collective-permute-done((bf16[12,128,128]{2,1,0:T(8,128)(2,1)S(1)}, bf16[12,128,128]{2,1,0:T(8,128)(2,1)S(1)}, u32[]{:S(2)}, u32[]{:S(2)}) %collective-permute-start.1) | collective-permute-done | bytes 393248 | tf_op jit(solution)/shard_map/ppermute | solution.py:460
  26.7 2.4 %collective-permute-start.9 = (bf16[4,128,128]{2,1,0:T(8,128)(2,1)S(1)}, bf16[4,128,128]{2,1,0:T(8,128)(2,1)S(1)}, u32[]{:S(2)}, u32[]{:S(2)}) collective-permute-start(bf16[4,128,128]{2,1,0:T(8,128)(2,1)S(1)} %get-tuple-element.40), channel_id=1, source_target_pairs={{0,24},{4,28},{8,16},{12,20},{16,8},{20,12},{24,0},{28,4},{1,25},{... | collective-permute-start | bytes 393224 | tf_op jit(solution)/shard_map/ppermute | solution.py:460
  29.1 0.6 collective-permute-start.10
  29.7 0.5 collective-permute-start.11
  30.2 3.7 %apply_filter.2 = (bf16[12,128,128]{2,1,0:T(8,128)(2,1)S(1)}, bf16[12,128,128]{2,1,0:T(8,128)(2,1)S(1)}, bf16[12,128,128]{2,1,0:T(8,128)(2,1)S(1)}, bf16[12,128,128]{2,1,0:T(8,128)(2,1)S(1)}) custom-call(bf16[512,1024]{1,0:T(8,128)(2,1)S(1)} %get-tuple-element.25.refs_4_.high_ref, bf16[512,1024]{1,0:T(8,128)(2,1)S(1)} %get-tuple-element.26.low_ref, ...), custom_call_target="tpu_custom_call" | custom-call | tf_op jit(solution)/shard_map/apply_filter/pallas_call | solution.py:378
  34.0 2.4 %collective-permute-start.6 = (bf16[12,128,128]{2,1,0:T(8,128)(2,1)S(1)}, bf16[12,128,128]{2,1,0:T(8,128)(2,1)S(1)}, u32[]{:S(2)}, u32[]{:S(2)}) collective-permute-start(bf16[12,128,128]{2,1,0:T(8,128)(2,1)S(1)} %get-tuple-element.37), channel_id=1, source_target_pairs={{0,24},{4,28},{8,16},{12,20},{16,8},{20,12},{24,0},{28,4},{1,25},{... | collective-permute-start | bytes 1179656 | tf_op jit(solution)/shard_map/ppermute | solution.py:460
  36.4 0.6 collective-permute-start.7
  37.0 0.5 collective-permute-start.8
  37.7 4.6 %all_to_all.10.refs_0_ = bf16[2,512,512]{2,1,0:T(8,128)(2,1)S(1)} all-to-all(bf16[2,512,512]{2,1,0:T(8,128)(2,1)S(1)} %pack.3), channel_id=1, replica_groups={{0,4},{8,12},{16,20},{24,28},{1,5},{9,13},{17,21},{25,29},{2,6},{10,14}..., dimensions={0} | all-to-all | bytes 2097152 | tf_op jit(solution)/shard_map/all_to_all | solution.py:486
  42.3 2.3 %apply_filter.3 = bf16[4,4,128,128]{3,2,1,0:T(8,128)(2,1)} custom-call(bf16[512,1024]{1,0:T(8,128)(2,1)S(1)} %get-tuple-element.25.refs_4_.high_ref, bf16[512,1024]{1,0:T(8,128)(2,1)S(1)} %get-tuple-element.26.low_ref, bf16[2,512,512]{2,1,0:T(8,128)(2,1)S(1)} %all_to_all.10.refs_0_), custom_call_target="tpu_custom_call" | custom-call | tf_op jit(solution)/shard_map/apply_filter/pallas_call | solution.py:378
  44.6 3.6 %all-to-all-start.1 = ((bf16[4,4,128,128]{3,2,1,0:T(8,128)(2,1)}), bf16[4,4,128,128]{3,2,1,0:T(8,128)(2,1)S(1)}, u32[]{:S(2)}, u32[]{:S(2)}) async-start(bf16[4,4,128,128]{3,2,1,0:T(8,128)(2,1)} %apply_filter.3), calls=%async_computation.1 | async-start | bytes 1048576 | tf_op jit(solution)/shard_map/all_to_all | solution.py:489
  48.2 7.3 %collective-permute-done.7.refs_2_ = bf16[12,128,128]{2,1,0:T(8,128)(2,1)S(1)} collective-permute-done((bf16[12,128,128]{2,1,0:T(8,128)(2,1)S(1)}, bf16[12,128,128]{2,1,0:T(8,128)(2,1)S(1)}, u32[]{:S(2)}, u32[]{:S(2)}) %collective-permute-start.7) | collective-permute-done | bytes 393248 | tf_op jit(solution)/shard_map/ppermute | solution.py:460
  55.5 4.5 %all-to-all-done.1.refs_4_ = bf16[4,4,128,128]{3,2,1,0:T(8,128)(2,1)S(1)} async-done(((bf16[4,4,128,128]{3,2,1,0:T(8,128)(2,1)}), bf16[4,4,128,128]{3,2,1,0:T(8,128)(2,1)S(1)}, u32[]{:S(2)}, u32[]{:S(2)}) %all-to-all-start.1) | async-done | bytes 524320 | tf_op jit(solution)/shard_map/all_to_all | solution.py:489
  60.0 3.4 %anomaly.1 = f32[2,1024,512]{2,1,0:T(8,128)} custom-call(bf16[3,1408,512]{2,1,0:T(8,128)(2,1)} %copy-done, bf16[12,128,128]{2,1,0:T(8,128)(2,1)S(1)} %get-tuple-element.36.refs_4_.refs_0_, bf16[12,128,128]{2,1,0:T(8,128)(2,1)S(1)} %collective-permute-done.6.refs_1_, bf16[12,128,128]{2,1,0:T(8,128)(2,1)S(1)} %collective-permute-done.7.refs_2_, ...), custom_call_target="tpu_custom_call" | custom-call | tf_op jit(solution)/shard_map/anomaly/pallas_call | solution.py:440
  (20 shorter events, 1.4 us)
Async XLA Ops:
  0.0 14.4 %copy-start.1 = (s32[256]{0:T(256)S(1)}, s32[256]{0:T(256)}, u32[]{:S(2)}) copy-start(s32[256]{0:T(256)} %param.5) | copy-start | bytes 3076
  4.5 19.1 %copy-start = (bf16[3,1408,512]{2,1,0:T(8,128)(2,1)}, bf16[3,1408,512]{2,1,0:T(8,128)(2,1)S(1)}, u32[]{:S(2)}) copy-start(bf16[3,1408,512]{2,1,0:T(8,128)(2,1)S(1)} %get-tuple-element.24.masked_ref) | copy-start | bytes 12976132
  4.5 19.1 %collective-permute-start = (bf16[12,128,128]{2,1,0:T(8,128)(2,1)S(1)}, bf16[12,128,128]{2,1,0:T(8,128)(2,1)S(1)}, u32[]{:S(2)}, u32[]{:S(2)}) collective-permute-start(bf16[12,128,128]{2,1,0:T(8,128)(2,1)S(1)} %get-tuple-element.28), channel_id=1, source_target_pairs={{0,24},{4,28},{8,16},{12,20},{16,8},{20,12},{24,0},{28,4},{1,25},{... | collective-permute-start | bytes 1179656 | tf_op jit(solution)/shard_map/ppermute | solution.py:460
  8.5 17.5 %collective-permute-start.1 = (bf16[12,128,128]{2,1,0:T(8,128)(2,1)S(1)}, bf16[12,128,128]{2,1,0:T(8,128)(2,1)S(1)}, u32[]{:S(2)}, u32[]{:S(2)}) collective-permute-start(bf16[12,128,128]{2,1,0:T(8,128)(2,1)S(1)} %get-tuple-element.29), channel_id=1, source_target_pairs={{0,16},{4,12},{8,24},{12,4},{16,0},{20,28},{24,8},{28,20},{1,17},{... | collective-permute-start | bytes 1179656 | tf_op jit(solution)/shard_map/ppermute | solution.py:460
  9.0 17.3 %collective-permute-start.2 = (bf16[12,128,128]{2,1,0:T(8,128)(2,1)S(1)}, bf16[12,128,128]{2,1,0:T(8,128)(2,1)S(1)}, u32[]{:S(2)}, u32[]{:S(2)}) collective-permute-start(bf16[12,128,128]{2,1,0:T(8,128)(2,1)S(1)} %get-tuple-element.30), channel_id=1, source_target_pairs={{0,8},{4,20},{8,0},{12,28},{16,24},{20,4},{24,16},{28,12},{1,9},{5... | collective-permute-start | bytes 1179656 | tf_op jit(solution)/shard_map/ppermute | solution.py:460
  9.2 9.3 %collective-permute-start.3 = (bf16[9,128,128]{2,1,0:T(8,128)(2,1)S(1)}, bf16[9,128,128]{2,1,0:T(8,128)(2,1)S(1)}, u32[]{:S(2)}, u32[]{:S(2)}) collective-permute-start(bf16[9,128,128]{2,1,0:T(8,128)(2,1)S(1)} %get-tuple-element.33), channel_id=1, source_target_pairs={{0,1},{1,2},{2,3},{4,5},{5,6},{6,7},{8,9},{9,10},{10,11},{12,13},{... | collective-permute-start | bytes 884744 | tf_op jit(solution)/shard_map/ppermute | solution.py:476
  13.1 9.5 %collective-permute-start.4 = (bf16[9,128,128]{2,1,0:T(8,128)(2,1)S(1)}, bf16[9,128,128]{2,1,0:T(8,128)(2,1)S(1)}, u32[]{:S(2)}, u32[]{:S(2)}) collective-permute-start(bf16[9,128,128]{2,1,0:T(8,128)(2,1)S(1)} %get-tuple-element.34), channel_id=1, source_target_pairs={{1,0},{2,1},{3,2},{5,4},{6,5},{7,6},{9,8},{10,9},{11,10},{13,12},{... | collective-permute-start | bytes 884744 | tf_op jit(solution)/shard_map/ppermute | solution.py:477
  26.6 3.6 %collective-permute-start.5 = (bf16[512,1536]{1,0:T(8,128)(2,1)S(1)}, bf16[512,1536]{1,0:T(8,128)(2,1)S(1)}, u32[]{:S(2)}, u32[]{:S(2)}) collective-permute-start(bf16[512,1536]{1,0:T(8,128)(2,1)S(1)} %pack.2.refs_0_), channel_id=1, source_target_pairs={{0,4},{4,0},{8,12},{12,8},{16,20},{20,16},{24,28},{28,24},{1,5},{5... | collective-permute-start | bytes 4718600 | tf_op jit(solution)/shard_map/ppermute | solution.py:482
  26.7 10.3 %collective-permute-start.9 = (bf16[4,128,128]{2,1,0:T(8,128)(2,1)S(1)}, bf16[4,128,128]{2,1,0:T(8,128)(2,1)S(1)}, u32[]{:S(2)}, u32[]{:S(2)}) collective-permute-start(bf16[4,128,128]{2,1,0:T(8,128)(2,1)S(1)} %get-tuple-element.40), channel_id=1, source_target_pairs={{0,24},{4,28},{8,16},{12,20},{16,8},{20,12},{24,0},{28,4},{1,25},{... | collective-permute-start | bytes 393224 | tf_op jit(solution)/shard_map/ppermute | solution.py:460
  29.1 8.4 %collective-permute-start.10 = (bf16[4,128,128]{2,1,0:T(8,128)(2,1)S(1)}, bf16[4,128,128]{2,1,0:T(8,128)(2,1)S(1)}, u32[]{:S(2)}, u32[]{:S(2)}) collective-permute-start(bf16[4,128,128]{2,1,0:T(8,128)(2,1)S(1)} %get-tuple-element.41), channel_id=1, source_target_pairs={{0,16},{4,12},{8,24},{12,4},{16,0},{20,28},{24,8},{28,20},{1,17},{... | collective-permute-start | bytes 393224 | tf_op jit(solution)/shard_map/ppermute | solution.py:460
  29.7 7.8 %collective-permute-start.11 = (bf16[4,128,128]{2,1,0:T(8,128)(2,1)S(1)}, bf16[4,128,128]{2,1,0:T(8,128)(2,1)S(1)}, u32[]{:S(2)}, u32[]{:S(2)}) collective-permute-start(bf16[4,128,128]{2,1,0:T(8,128)(2,1)S(1)} %get-tuple-element.42), channel_id=1, source_target_pairs={{0,8},{4,20},{8,0},{12,28},{16,24},{20,4},{24,16},{28,12},{1,9},{5... | collective-permute-start | bytes 393224 | tf_op jit(solution)/shard_map/ppermute | solution.py:460
  34.0 14.2 %collective-permute-start.6 = (bf16[12,128,128]{2,1,0:T(8,128)(2,1)S(1)}, bf16[12,128,128]{2,1,0:T(8,128)(2,1)S(1)}, u32[]{:S(2)}, u32[]{:S(2)}) collective-permute-start(bf16[12,128,128]{2,1,0:T(8,128)(2,1)S(1)} %get-tuple-element.37), channel_id=1, source_target_pairs={{0,24},{4,28},{8,16},{12,20},{16,8},{20,12},{24,0},{28,4},{1,25},{... | collective-permute-start | bytes 1179656 | tf_op jit(solution)/shard_map/ppermute | solution.py:460
  36.4 19.0 %collective-permute-start.7 = (bf16[12,128,128]{2,1,0:T(8,128)(2,1)S(1)}, bf16[12,128,128]{2,1,0:T(8,128)(2,1)S(1)}, u32[]{:S(2)}, u32[]{:S(2)}) collective-permute-start(bf16[12,128,128]{2,1,0:T(8,128)(2,1)S(1)} %get-tuple-element.38), channel_id=1, source_target_pairs={{0,16},{4,12},{8,24},{12,4},{16,0},{20,28},{24,8},{28,20},{1,17},{... | collective-permute-start | bytes 1179656 | tf_op jit(solution)/shard_map/ppermute | solution.py:460
  37.0 18.5 %collective-permute-start.8 = (bf16[12,128,128]{2,1,0:T(8,128)(2,1)S(1)}, bf16[12,128,128]{2,1,0:T(8,128)(2,1)S(1)}, u32[]{:S(2)}, u32[]{:S(2)}) collective-permute-start(bf16[12,128,128]{2,1,0:T(8,128)(2,1)S(1)} %get-tuple-element.39), channel_id=1, source_target_pairs={{0,8},{4,20},{8,0},{12,28},{16,24},{20,4},{24,16},{28,12},{1,9},{5... | collective-permute-start | bytes 1179656 | tf_op jit(solution)/shard_map/ppermute | solution.py:460
  44.6 15.4 %all-to-all-start.1 = ((bf16[4,4,128,128]{3,2,1,0:T(8,128)(2,1)}), bf16[4,4,128,128]{3,2,1,0:T(8,128)(2,1)S(1)}, u32[]{:S(2)}, u32[]{:S(2)}) async-start(bf16[4,4,128,128]{3,2,1,0:T(8,128)(2,1)} %apply_filter.3), calls=%async_computation.1 | async-start | bytes 1048576 | tf_op jit(solution)/shard_map/all_to_all | solution.py:489

commit v3 on v2

--- a/solution.py
+++ b/solution.py
@@ -347,28 +347,21 @@
 
 
 def apply_kernel(chips, shared, high_ref, low_ref, *refs):
-    outs, result = refs[-2] if shared else refs[-1 - chips : -1], refs[-1]
+    outs = refs[-1] if shared else refs[-chips:]
     units, dates, lanes = outs.shape[1:] if shared else outs[0].shape
     half = high_ref.shape[0]
-    chip, core = lax.axis_index(DATE) // 2, lax.axis_index(DATE) % 2
+    core = lax.axis_index(DATE) % 2
     own_ref, other_ref = (refs[0].at[core], refs[0].at[1 - core]) if shared else refs[:2]
-    tile = min(half, 256)
-
-    @pl.loop(0, half // tile)
-    def _(step):
-        at = pl.ds(pl.multiple_of(step * tile, tile), tile)
+    for m in range(chips):
+        at = pl.ds(m * dates if shared else pl.multiple_of(partner(m, chips) * dates, dates), dates)
+        out = outs.at[m] if shared else outs[m]
         total = None
         for ref in (high_ref, low_ref):
             for series, left in ((own_ref, 0), (other_ref, half)):
                 part = product(ref[at, left : left + half], series[...])
                 total = part if total is None else total + part
-        result[at, :] = total
-
-    for m in range(chips):
-        at = m * dates if shared else pl.multiple_of(partner(m, chips) * dates, dates)
-        out = outs.at[m] if shared else outs[m]
         for i in range(units):
-            out[i] = result[pl.ds(at, dates), i * lanes : (i + 1) * lanes].astype(jnp.bfloat16)
+            out[i] = total[:, i * lanes : (i + 1) * lanes].astype(jnp.bfloat16)
 
 
 def apply_filter(high, low, series, chips):
@@ -378,7 +371,6 @@
     return pl.pallas_call(
         functools.partial(apply_kernel, chips, shared),
         out_shape=jax.ShapeDtypeStruct((chips, *piece.shape), piece.dtype) if shared else [piece] * chips,
-        scratch_shapes=[pltpu.VMEM((half, width), jnp.float32)],
         compiler_params=pltpu.CompilerParams(vmem_limit_bytes=16 * MIB),
         name="apply_filter",
     )(high, low, *series)

time: 63.7 us -> 63.4 us (level)
  transfers between devices with their start and end apart: 13 -> 13, of which waited for: 6 -> 6; matrix products, arithmetic and copies ran while one was open for 2% -> 2% of each run, Pallas kernels for 12% -> 11%
where the time goes in v3:
time: 63.4 us; the launch traced here: 63.1 us
  waiting for transfers between devices  21.6 us (34%)
  starting transfers between devices  20.6 us (32%)
  Pallas kernels  15.3 us (24%)
  blocking collectives  4.58 us (7%)
  other arithmetic  0.72 us (1%)
    ppermute x9, starting transfers between devices, exchange(): out[m] = lax.ppermute(pieces[m], DATE, to)  11.7 us
    ppermute x9, waiting for transfers between devices, exchange(): out[m] = lax.ppermute(pieces[m], DATE, to)  10.2 us
    pallas_call x2, Pallas kernels, apply_filter(): pl.pallas_call(functools.partial(apply_kernel, chips, shared), out_shape=...  5.47 us
    all_to_all x1, blocking collectives, on_device(): lax.all_to_all(own, DATE, 0, 0, axis_index_groups=[[i, i + 1] for i in ra...  4.58 us
    all_to_all x1, waiting for transfers between devices, on_device(): results.append(lax.all_to_all(made, DATE, 0, 0, axis_index_groups=cores))  4.53 us
    pallas_call x1, Pallas kernels, smooth_first(): pl.pallas_call(functools.partial(first_kernel, chunks, chips), in_specs=[...  4.51 us
    ppermute x1, waiting for transfers between devices, on_device(): after = lax.ppermute(first, TILE, [(j, i) for i, j in up])  4.13 us
    ppermute x1, starting transfers between devices, on_device(): before = lax.ppermute(last, TILE, up)  3.89 us
  transfers between devices with their start and end apart: 13, of which 6 were waited for; matrix products, arithmetic and copies ran while one was open for 2% of the time, Pallas kernels for 11%

profile of v3, /device:TPU:0, one launch (start us, length us, event | category | flops | bytes accessed | tf_op | source)
XLA Modules:
  0.0 63.1 jit_solution(8399319700254770671)
XLA Ops:
  0.0 4.5 %smooth_first.1 = (bf16[12,128,128]{2,1,0:T(8,128)(2,1)S(1)}, bf16[12,128,128]{2,1,0:T(8,128)(2,1)S(1)}, bf16[12,128,128]{2,1,0:T(8,128)(2,1)S(1)}, bf16[12,128,...) custom-call(bf16[2,1024,512]{2,1,0:T(8,128)(2,1)} %bitcast.3, ...), custom_call_target="tpu_custom_call" | custom-call | tf_op jit(solution)/shard_map/smooth_first/pallas_call | solution.py:206
  4.5 4.0 %collective-permute-start = (bf16[12,128,128]{2,1,0:T(8,128)(2,1)S(1)}, bf16[12,128,128]{2,1,0:T(8,128)(2,1)S(1)}, u32[]{:S(2)}, u32[]{:S(2)}) collective-permute-start(bf16[12,128,128]{2,1,0:T(8,128)(2,1)S(1)} %get-tuple-element.28), channel_id=1, source_target_pairs={{0,24},{4,28},{8,16},{12,20},{16,8},{20,12},{24,0},{28,4},{1,25},{... | collective-permute-start | bytes 1179656 | tf_op jit(solution)/shard_map/ppermute | solution.py:452
  8.5 0.5 collective-permute-start.1
  9.2 3.9 %collective-permute-start.3 = (bf16[9,128,128]{2,1,0:T(8,128)(2,1)S(1)}, bf16[9,128,128]{2,1,0:T(8,128)(2,1)S(1)}, u32[]{:S(2)}, u32[]{:S(2)}) collective-permute-start(bf16[9,128,128]{2,1,0:T(8,128)(2,1)S(1)} %get-tuple-element.33), channel_id=1, source_target_pairs={{0,1},{1,2},{2,3},{4,5},{5,6},{6,7},{8,9},{9,10},{10,11},{12,13},{... | collective-permute-start | bytes 884744 | tf_op jit(solution)/shard_map/ppermute | solution.py:468
  13.1 1.3 %collective-permute-start.4 = (bf16[9,128,128]{2,1,0:T(8,128)(2,1)S(1)}, bf16[9,128,128]{2,1,0:T(8,128)(2,1)S(1)}, u32[]{:S(2)}, u32[]{:S(2)}) collective-permute-start(bf16[9,128,128]{2,1,0:T(8,128)(2,1)S(1)} %get-tuple-element.34), channel_id=1, source_target_pairs={{1,0},{2,1},{3,2},{5,4},{6,5},{7,6},{9,8},{10,9},{11,10},{13,12},{... | collective-permute-start | bytes 884744 | tf_op jit(solution)/shard_map/ppermute | solution.py:469
  14.4 0.6 fusion.9
  15.4 0.4 filter_matrix.1
  15.7 2.7 %collective-permute-done.3.before_ref = bf16[9,128,128]{2,1,0:T(8,128)(2,1)S(1)} collective-permute-done((bf16[9,128,128]{2,1,0:T(8,128)(2,1)S(1)}, bf16[9,128,128]{2,1,0:T(8,128)(2,1)S(1)}, u32[]{:S(2)}, u32[]{:S(2)}) %collective-permute-start.3) | collective-permute-done | bytes 294944 | tf_op jit(solution)/shard_map/ppermute | solution.py:468
  18.5 4.1 %collective-permute-done.4.after_ref = bf16[9,128,128]{2,1,0:T(8,128)(2,1)S(1)} collective-permute-done((bf16[9,128,128]{2,1,0:T(8,128)(2,1)S(1)}, bf16[9,128,128]{2,1,0:T(8,128)(2,1)S(1)}, u32[]{:S(2)}, u32[]{:S(2)}) %collective-permute-start.4) | collective-permute-done | bytes 294944 | tf_op jit(solution)/shard_map/ppermute | solution.py:469
  22.6 1.0 %smooth_rest.1 = (bf16[4,128,128]{2,1,0:T(8,128)(2,1)S(1)}, bf16[4,128,128]{2,1,0:T(8,128)(2,1)S(1)}, bf16[4,128,128]{2,1,0:T(8,128)(2,1)S(1)}, bf16[4,128,128]{2,1,0:T(8,128)(2,1)S(1)}) custom-call(bf16[3,1408,512]{2,1,0:T(8,128)(2,1)S(1)} %get-tuple-element.24.masked_ref, bf16[9,128,128]{2,1,0:T(8,128)(2,1)S(1)} %collective-permute-done.3.before_ref, ...), custom_call_target="tpu_custom_call" | custom-call | tf_op jit(solution)/shard_map/smooth_rest/pallas_call | solution.py:269
  23.6 2.4 %collective-permute-done.1.refs_2_ = bf16[12,128,128]{2,1,0:T(8,128)(2,1)S(1)} collective-permute-done((bf16[12,128,128]{2,1,0:T(8,128)(2,1)S(1)}, bf16[12,128,128]{2,1,0:T(8,128)(2,1)S(1)}, u32[]{:S(2)}, u32[]{:S(2)}) %collective-permute-start.1) | collective-permute-done | bytes 393248 | tf_op jit(solution)/shard_map/ppermute | solution.py:452
  26.7 2.4 %collective-permute-start.9 = (bf16[4,128,128]{2,1,0:T(8,128)(2,1)S(1)}, bf16[4,128,128]{2,1,0:T(8,128)(2,1)S(1)}, u32[]{:S(2)}, u32[]{:S(2)}) collective-permute-start(bf16[4,128,128]{2,1,0:T(8,128)(2,1)S(1)} %get-tuple-element.40), channel_id=1, source_target_pairs={{0,24},{4,28},{8,16},{12,20},{16,8},{20,12},{24,0},{28,4},{1,25},{... | collective-permute-start | bytes 393224 | tf_op jit(solution)/shard_map/ppermute | solution.py:452
  29.1 0.6 collective-permute-start.10
  29.7 0.5 collective-permute-start.11
  30.2 3.4 %apply_filter.2 = (bf16[12,128,128]{2,1,0:T(8,128)(2,1)S(1)}, bf16[12,128,128]{2,1,0:T(8,128)(2,1)S(1)}, bf16[12,128,128]{2,1,0:T(8,128)(2,1)S(1)}, bf16[12,128,128]{2,1,0:T(8,128)(2,1)S(1)}) custom-call(bf16[512,1024]{1,0:T(8,128)(2,1)S(1)} %get-tuple-element.25.refs_4_.high_ref, bf16[512,1024]{1,0:T(8,128)(2,1)S(1)} %get-tuple-element.26.low_ref, ...), custom_call_target="tpu_custom_call" | custom-call | tf_op jit(solution)/shard_map/apply_filter/pallas_call | solution.py:371
  33.7 2.4 %collective-permute-start.6 = (bf16[12,128,128]{2,1,0:T(8,128)(2,1)S(1)}, bf16[12,128,128]{2,1,0:T(8,128)(2,1)S(1)}, u32[]{:S(2)}, u32[]{:S(2)}) collective-permute-start(bf16[12,128,128]{2,1,0:T(8,128)(2,1)S(1)} %get-tuple-element.37), channel_id=1, source_target_pairs={{0,24},{4,28},{8,16},{12,20},{16,8},{20,12},{24,0},{28,4},{1,25},{... | collective-permute-start | bytes 1179656 | tf_op jit(solution)/shard_map/ppermute | solution.py:452
  36.1 0.6 collective-permute-start.7
  36.7 0.5 collective-permute-start.8
  37.4 4.6 %all_to_all.10.refs_0_ = bf16[2,512,512]{2,1,0:T(8,128)(2,1)S(1)} all-to-all(bf16[2,512,512]{2,1,0:T(8,128)(2,1)S(1)} %pack.3), channel_id=1, replica_groups={{0,4},{8,12},{16,20},{24,28},{1,5},{9,13},{17,21},{25,29},{2,6},{10,14}..., dimensions={0} | all-to-all | bytes 2097152 | tf_op jit(solution)/shard_map/all_to_all | solution.py:478
  42.0 2.1 %apply_filter.3 = bf16[4,4,128,128]{3,2,1,0:T(8,128)(2,1)} custom-call(bf16[512,1024]{1,0:T(8,128)(2,1)S(1)} %get-tuple-element.25.refs_4_.high_ref, bf16[512,1024]{1,0:T(8,128)(2,1)S(1)} %get-tuple-element.26.low_ref, bf16[2,512,512]{2,1,0:T(8,128)(2,1)S(1)} %all_to_all.10.refs_0_), custom_call_target="tpu_custom_call" | custom-call | tf_op jit(solution)/shard_map/apply_filter/pallas_call | solution.py:371
  44.0 3.6 %all-to-all-start.1 = ((bf16[4,4,128,128]{3,2,1,0:T(8,128)(2,1)}), bf16[4,4,128,128]{3,2,1,0:T(8,128)(2,1)S(1)}, u32[]{:S(2)}, u32[]{:S(2)}) async-start(bf16[4,4,128,128]{3,2,1,0:T(8,128)(2,1)} %apply_filter.3), calls=%async_computation.1 | async-start | bytes 1048576 | tf_op jit(solution)/shard_map/all_to_all | solution.py:481
  47.7 7.5 %collective-permute-done.7.refs_2_ = bf16[12,128,128]{2,1,0:T(8,128)(2,1)S(1)} collective-permute-done((bf16[12,128,128]{2,1,0:T(8,128)(2,1)S(1)}, bf16[12,128,128]{2,1,0:T(8,128)(2,1)S(1)}, u32[]{:S(2)}, u32[]{:S(2)}) %collective-permute-start.7) | collective-permute-done | bytes 393248 | tf_op jit(solution)/shard_map/ppermute | solution.py:452
  55.1 4.5 %all-to-all-done.1.refs_4_ = bf16[4,4,128,128]{3,2,1,0:T(8,128)(2,1)S(1)} async-done(((bf16[4,4,128,128]{3,2,1,0:T(8,128)(2,1)}), bf16[4,4,128,128]{3,2,1,0:T(8,128)(2,1)S(1)}, u32[]{:S(2)}, u32[]{:S(2)}) %all-to-all-start.1) | async-done | bytes 524320 | tf_op jit(solution)/shard_map/all_to_all | solution.py:481
  59.7 3.4 %anomaly.1 = f32[2,1024,512]{2,1,0:T(8,128)} custom-call(bf16[3,1408,512]{2,1,0:T(8,128)(2,1)} %copy-done, bf16[12,128,128]{2,1,0:T(8,128)(2,1)S(1)} %get-tuple-element.36.refs_4_.refs_0_, bf16[12,128,128]{2,1,0:T(8,128)(2,1)S(1)} %collective-permute-done.6.refs_1_, bf16[12,128,128]{2,1,0:T(8,128)(2,1)S(1)} %collective-permute-done.7.refs_2_, ...), custom_call_target="tpu_custom_call" | custom-call | tf_op jit(solution)/shard_map/anomaly/pallas_call | solution.py:432
  (20 shorter events, 1.4 us)
Async XLA Ops:
  0.0 14.4 %copy-start.1 = (s32[256]{0:T(256)S(1)}, s32[256]{0:T(256)}, u32[]{:S(2)}) copy-start(s32[256]{0:T(256)} %param.5) | copy-start | bytes 3076
  4.5 19.1 %copy-start = (bf16[3,1408,512]{2,1,0:T(8,128)(2,1)}, bf16[3,1408,512]{2,1,0:T(8,128)(2,1)S(1)}, u32[]{:S(2)}) copy-start(bf16[3,1408,512]{2,1,0:T(8,128)(2,1)S(1)} %get-tuple-element.24.masked_ref) | copy-start | bytes 12976132
  4.5 19.1 %collective-permute-start = (bf16[12,128,128]{2,1,0:T(8,128)(2,1)S(1)}, bf16[12,128,128]{2,1,0:T(8,128)(2,1)S(1)}, u32[]{:S(2)}, u32[]{:S(2)}) collective-permute-start(bf16[12,128,128]{2,1,0:T(8,128)(2,1)S(1)} %get-tuple-element.28), channel_id=1, source_target_pairs={{0,24},{4,28},{8,16},{12,20},{16,8},{20,12},{24,0},{28,4},{1,25},{... | collective-permute-start | bytes 1179656 | tf_op jit(solution)/shard_map/ppermute | solution.py:452
  8.5 17.5 %collective-permute-start.1 = (bf16[12,128,128]{2,1,0:T(8,128)(2,1)S(1)}, bf16[12,128,128]{2,1,0:T(8,128)(2,1)S(1)}, u32[]{:S(2)}, u32[]{:S(2)}) collective-permute-start(bf16[12,128,128]{2,1,0:T(8,128)(2,1)S(1)} %get-tuple-element.29), channel_id=1, source_target_pairs={{0,16},{4,12},{8,24},{12,4},{16,0},{20,28},{24,8},{28,20},{1,17},{... | collective-permute-start | bytes 1179656 | tf_op jit(solution)/shard_map/ppermute | solution.py:452
  9.0 17.3 %collective-permute-start.2 = (bf16[12,128,128]{2,1,0:T(8,128)(2,1)S(1)}, bf16[12,128,128]{2,1,0:T(8,128)(2,1)S(1)}, u32[]{:S(2)}, u32[]{:S(2)}) collective-permute-start(bf16[12,128,128]{2,1,0:T(8,128)(2,1)S(1)} %get-tuple-element.30), channel_id=1, source_target_pairs={{0,8},{4,20},{8,0},{12,28},{16,24},{20,4},{24,16},{28,12},{1,9},{5... | collective-permute-start | bytes 1179656 | tf_op jit(solution)/shard_map/ppermute | solution.py:452
  9.2 9.3 %collective-permute-start.3 = (bf16[9,128,128]{2,1,0:T(8,128)(2,1)S(1)}, bf16[9,128,128]{2,1,0:T(8,128)(2,1)S(1)}, u32[]{:S(2)}, u32[]{:S(2)}) collective-permute-start(bf16[9,128,128]{2,1,0:T(8,128)(2,1)S(1)} %get-tuple-element.33), channel_id=1, source_target_pairs={{0,1},{1,2},{2,3},{4,5},{5,6},{6,7},{8,9},{9,10},{10,11},{12,13},{... | collective-permute-start | bytes 884744 | tf_op jit(solution)/shard_map/ppermute | solution.py:468
  13.1 9.5 %collective-permute-start.4 = (bf16[9,128,128]{2,1,0:T(8,128)(2,1)S(1)}, bf16[9,128,128]{2,1,0:T(8,128)(2,1)S(1)}, u32[]{:S(2)}, u32[]{:S(2)}) collective-permute-start(bf16[9,128,128]{2,1,0:T(8,128)(2,1)S(1)} %get-tuple-element.34), channel_id=1, source_target_pairs={{1,0},{2,1},{3,2},{5,4},{6,5},{7,6},{9,8},{10,9},{11,10},{13,12},{... | collective-permute-start | bytes 884744 | tf_op jit(solution)/shard_map/ppermute | solution.py:469
  26.6 3.6 %collective-permute-start.5 = (bf16[512,1536]{1,0:T(8,128)(2,1)S(1)}, bf16[512,1536]{1,0:T(8,128)(2,1)S(1)}, u32[]{:S(2)}, u32[]{:S(2)}) collective-permute-start(bf16[512,1536]{1,0:T(8,128)(2,1)S(1)} %pack.2.refs_0_), channel_id=1, source_target_pairs={{0,4},{4,0},{8,12},{12,8},{16,20},{20,16},{24,28},{28,24},{1,5},{5... | collective-permute-start | bytes 4718600 | tf_op jit(solution)/shard_map/ppermute | solution.py:474
  26.7 10.0 %collective-permute-start.9 = (bf16[4,128,128]{2,1,0:T(8,128)(2,1)S(1)}, bf16[4,128,128]{2,1,0:T(8,128)(2,1)S(1)}, u32[]{:S(2)}, u32[]{:S(2)}) collective-permute-start(bf16[4,128,128]{2,1,0:T(8,128)(2,1)S(1)} %get-tuple-element.40), channel_id=1, source_target_pairs={{0,24},{4,28},{8,16},{12,20},{16,8},{20,12},{24,0},{28,4},{1,25},{... | collective-permute-start | bytes 393224 | tf_op jit(solution)/shard_map/ppermute | solution.py:452
  29.1 8.1 %collective-permute-start.10 = (bf16[4,128,128]{2,1,0:T(8,128)(2,1)S(1)}, bf16[4,128,128]{2,1,0:T(8,128)(2,1)S(1)}, u32[]{:S(2)}, u32[]{:S(2)}) collective-permute-start(bf16[4,128,128]{2,1,0:T(8,128)(2,1)S(1)} %get-tuple-element.41), channel_id=1, source_target_pairs={{0,16},{4,12},{8,24},{12,4},{16,0},{20,28},{24,8},{28,20},{1,17},{... | collective-permute-start | bytes 393224 | tf_op jit(solution)/shard_map/ppermute | solution.py:452
  29.7 7.5 %collective-permute-start.11 = (bf16[4,128,128]{2,1,0:T(8,128)(2,1)S(1)}, bf16[4,128,128]{2,1,0:T(8,128)(2,1)S(1)}, u32[]{:S(2)}, u32[]{:S(2)}) collective-permute-start(bf16[4,128,128]{2,1,0:T(8,128)(2,1)S(1)} %get-tuple-element.42), channel_id=1, source_target_pairs={{0,8},{4,20},{8,0},{12,28},{16,24},{20,4},{24,16},{28,12},{1,9},{5... | collective-permute-start | bytes 393224 | tf_op jit(solution)/shard_map/ppermute | solution.py:452
  33.7 14.0 %collective-permute-start.6 = (bf16[12,128,128]{2,1,0:T(8,128)(2,1)S(1)}, bf16[12,128,128]{2,1,0:T(8,128)(2,1)S(1)}, u32[]{:S(2)}, u32[]{:S(2)}) collective-permute-start(bf16[12,128,128]{2,1,0:T(8,128)(2,1)S(1)} %get-tuple-element.37), channel_id=1, source_target_pairs={{0,24},{4,28},{8,16},{12,20},{16,8},{20,12},{24,0},{28,4},{1,25},{... | collective-permute-start | bytes 1179656 | tf_op jit(solution)/shard_map/ppermute | solution.py:452
  36.1 19.0 %collective-permute-start.7 = (bf16[12,128,128]{2,1,0:T(8,128)(2,1)S(1)}, bf16[12,128,128]{2,1,0:T(8,128)(2,1)S(1)}, u32[]{:S(2)}, u32[]{:S(2)}) collective-permute-start(bf16[12,128,128]{2,1,0:T(8,128)(2,1)S(1)} %get-tuple-element.38), channel_id=1, source_target_pairs={{0,16},{4,12},{8,24},{12,4},{16,0},{20,28},{24,8},{28,20},{1,17},{... | collective-permute-start | bytes 1179656 | tf_op jit(solution)/shard_map/ppermute | solution.py:452
  36.7 18.5 %collective-permute-start.8 = (bf16[12,128,128]{2,1,0:T(8,128)(2,1)S(1)}, bf16[12,128,128]{2,1,0:T(8,128)(2,1)S(1)}, u32[]{:S(2)}, u32[]{:S(2)}) collective-permute-start(bf16[12,128,128]{2,1,0:T(8,128)(2,1)S(1)} %get-tuple-element.39), channel_id=1, source_target_pairs={{0,8},{4,20},{8,0},{12,28},{16,24},{20,4},{24,16},{28,12},{1,9},{5... | collective-permute-start | bytes 1179656 | tf_op jit(solution)/shard_map/ppermute | solution.py:452
  44.0 15.6 %all-to-all-start.1 = ((bf16[4,4,128,128]{3,2,1,0:T(8,128)(2,1)}), bf16[4,4,128,128]{3,2,1,0:T(8,128)(2,1)S(1)}, u32[]{:S(2)}, u32[]{:S(2)}) async-start(bf16[4,4,128,128]{3,2,1,0:T(8,128)(2,1)} %apply_filter.3), calls=%async_computation.1 | async-start | bytes 1048576 | tf_op jit(solution)/shard_map/all_to_all | solution.py:481

commit v4 on v3

--- a/solution.py
+++ b/solution.py
@@ -21,9 +21,9 @@
     return sum((bits >> k & 1) << (width - 1 - k) for k in range(width)) if core else bits
 
 
-def partner(m, chips):
+def partner(m, chips, side=0):
     me = lax.axis_index(DATE)
-    return (me // 2) ^ jnp.where(me % 2 == 0, apart(m, chips, 0), apart(m, chips, 1))
+    return (me // 2) ^ jnp.where(me % 2 == side, apart(m, chips, 0), apart(m, chips, 1))
 
 
 def padded(size):
@@ -276,7 +276,7 @@
     )(masked, *halo)
 
 
-def filter_kernel(dates, wave_ref, high_ref, low_ref):
+def filter_kernel(dates, wave_ref, high_ref, low_ref, turned):
     total = high_ref.shape[1]
     chips = total // dates // 2
     core = lax.axis_index(DATE) % 2
@@ -288,12 +288,14 @@
     for side, base in enumerate((same, other)):
         high = base.astype(jnp.bfloat16)
         low = (base - high.astype(jnp.float32)).astype(jnp.bfloat16)
-        for ref, part in ((high_ref, high), (low_ref, low)):
-            for q in range(chips):
-                for s in range(chips):
-                    at = (s - q) % chips * 2 * dates
-                    left = (side * chips + s) * dates
-                    ref[q * dates : (q + 1) * dates, left : left + dates] = part[:, at : at + dates]
+        for n, (ref, part) in enumerate(((high_ref, high), (low_ref, low))):
+            turned[2 * side + n] = part
+            for m in range(chips):
+                for q in range(chips):
+                    step = lax.rem(partner(m, chips, side) + chips - q, chips)
+                    at = pl.multiple_of(step * 2 * dates, LANES)
+                    left = (side * chips + m) * dates
+                    ref[q * dates : (q + 1) * dates, left : left + dates] = turned[2 * side + n, :, pl.ds(at, dates)]
 
 
 def filter_matrix(harmonics, dates, peers):
@@ -316,6 +318,7 @@
     return pl.pallas_call(
         functools.partial(filter_kernel, dates),
         out_shape=[jax.ShapeDtypeStruct((total // 2, total), jnp.bfloat16)] * 2,
+        scratch_shapes=[pltpu.VMEM((4, dates, total), jnp.bfloat16)],
         compiler_params=pltpu.CompilerParams(vmem_limit_bytes=10 * MIB),
         name="filter_matrix",
     )(wave)
@@ -324,9 +327,8 @@
 def pack_kernel(chips, *refs):
     pieces, out_ref = refs[:chips], refs[-1]
     units, dates, lanes = pieces[0].shape
-    chip = lax.axis_index(DATE) // 2
     for m in range(chips):
-        at = pl.multiple_of(partner(m, chips) * dates, dates)
+        at = m * dates
         for i in range(units):
             part = (pl.ds(at, dates), pl.ds(i * lanes, lanes))
             for side in ((0,), (1,)) if len(out_ref.shape) == 3 else ((),):
@@ -346,34 +348,58 @@
     )(*pieces, *after)
 
 
-def apply_kernel(chips, shared, high_ref, low_ref, *refs):
+def begin_kernel(high_ref, low_ref, *refs):
+    pieces, (result, series) = refs[:-2], refs[-2:]
+    units, dates, lanes = pieces[0].shape
+    for m, piece in enumerate(pieces):
+        for i in range(units):
+            series[m * dates : (m + 1) * dates, i * lanes : (i + 1) * lanes] = piece[i]
+    depth, tile = series.shape[0], dates
+    for at in range(0, result.shape[0], tile):
+        lines = pl.ds(at, tile)
+        result[lines, :] = product(high_ref[lines, :depth], series[...]) + product(low_ref[lines, :depth], series[...])
+
+
+def begin(high, low, pieces):
+    units, dates, lanes = pieces[0].shape
+    return pl.pallas_call(
+        begin_kernel,
+        out_shape=jax.ShapeDtypeStruct((high.shape[0], units * lanes), jnp.float32),
+        scratch_shapes=[pltpu.VMEM((len(pieces) * dates, units * lanes), jnp.bfloat16)],
+        compiler_params=pltpu.CompilerParams(vmem_limit_bytes=12 * MIB),
+        name="begin",
+    )(high, low, *pieces)
+
+
+def apply_kernel(chips, shared, done, high_ref, low_ref, *refs):
     outs = refs[-1] if shared else refs[-chips:]
     units, dates, lanes = outs.shape[1:] if shared else outs[0].shape
     half = high_ref.shape[0]
     core = lax.axis_index(DATE) % 2
     own_ref, other_ref = (refs[0].at[core], refs[0].at[1 - core]) if shared else refs[:2]
+    begun = done * dates
     for m in range(chips):
         at = pl.ds(m * dates if shared else pl.multiple_of(partner(m, chips) * dates, dates), dates)
         out = outs.at[m] if shared else outs[m]
-        total = None
+        total = refs[2][at, :] if done > 0 else None
         for ref in (high_ref, low_ref):
-            for series, left in ((own_ref, 0), (other_ref, half)):
-                part = product(ref[at, left : left + half], series[...])
+            for series, first, left in ((own_ref, begun, 0), (other_ref, 0, half)):
+                part = product(ref[at, left + first : left + half], series[first:half, :])
                 total = part if total is None else total + part
         for i in range(units):
             out[i] = total[:, i * lanes : (i + 1) * lanes].astype(jnp.bfloat16)
 
 
-def apply_filter(high, low, series, chips):
+def apply_filter(high, low, series, chips, begun=(), done=0):
     half, width = series[0].shape[-2:]
     piece = jax.ShapeDtypeStruct((width // LANES, half // chips, LANES), jnp.bfloat16)
     shared = len(series) == 1
     return pl.pallas_call(
-        functools.partial(apply_kernel, chips, shared),
+        functools.partial(apply_kernel, chips, shared, done),
         out_shape=jax.ShapeDtypeStruct((chips, *piece.shape), piece.dtype) if shared else [piece] * chips,
         compiler_params=pltpu.CompilerParams(vmem_limit_bytes=16 * MIB),
         name="apply_filter",
-    )(high, low, *series)
+    )(high, low, *series, *begun)
 
 
 def anomaly_kernel(chunks, chips, masked_ref, *refs):
@@ -470,9 +496,10 @@
     edges = smooth_rest(masked, height, (before, after), chunks[1], chips)
     outer = exchange(edges, peers)
     high, low = filter_matrix(harmonics, dates, peers)
-    own = pack(inner, (high, edges[0]), 1)
+    begun = begin(high, low, inner[:2])
+    own = pack(inner, (begun, edges[0]), 1)
     other = lax.ppermute(own, DATE, [(i, i ^ 1) for i in range(peers)])
-    made = apply_filter(high, low, (own, other), chips)
+    made = apply_filter(high, low, (own, other), chips, (begun,), 2)
     results = exchange(made, peers)
     own = pack(outer, (made[0],), 2)
     both = lax.all_to_all(own, DATE, 0, 0, axis_index_groups=[[i, i + 1] for i in range(0, peers, 2)])

time: 63.4 us -> 62.6 us (0.987)
  waiting for transfers between devices: 21.6 us -> 18.7 us
  other arithmetic: 0.72 us -> 2.08 us
  Pallas kernels: 15.3 us -> 16 us
    ppermute x1, waiting for transfers between devices: 2.74 us -> 0.91 us  [on_device(): before = lax.ppermute(last, TILE, up)]
    cos x2, other arithmetic: 0.72 us -> 2.08 us  [turned(): return (jnp.cos(angle), jnp.sin(angle))]
    ppermute x9, waiting for transfers between devices: 10.2 us -> 9.09 us  [exchange(): out[m] = lax.ppermute(pieces[m], DATE, to)]
    pallas_call x2 -> x3, Pallas kernels: 5.47 us -> 5.77 us  [the longest x2 4.66 us: apply_filter(): pl.pallas_call(functools.partial(apply_kernel, chips, shared, done), out_...]
  transfers between devices with their start and end apart: 13 -> 13, of which waited for: 6 -> 6; matrix products, arithmetic and copies ran while one was open for 2% -> 4% of each run, Pallas kernels for 11% -> 12%
where the time goes in v4:
time: 62.6 us; the launch traced here: 62.3 us
  starting transfers between devices  20.6 us (33%)
  waiting for transfers between devices  18.7 us (30%)
  Pallas kernels  16 us (26%)
  blocking collectives  4.58 us (7%)
  other arithmetic  2.08 us (3%)
    ppermute x9, starting transfers between devices, exchange(): out[m] = lax.ppermute(pieces[m], DATE, to)  11.7 us
    ppermute x9, waiting for transfers between devices, exchange(): out[m] = lax.ppermute(pieces[m], DATE, to)  9.09 us
    pallas_call x2, Pallas kernels, apply_filter(): pl.pallas_call(functools.partial(apply_kernel, chips, shared, done), out_...  4.66 us
    all_to_all x1, blocking collectives, on_device(): lax.all_to_all(own, DATE, 0, 0, axis_index_groups=[[i, i + 1] for i in ra...  4.58 us
    all_to_all x1, waiting for transfers between devices, on_device(): results.append(lax.all_to_all(made, DATE, 0, 0, axis_index_groups=cores))  4.54 us
    pallas_call x1, Pallas kernels, smooth_first(): pl.pallas_call(functools.partial(first_kernel, chunks, chips), in_specs=[...  4.5 us
    ppermute x1, waiting for transfers between devices, on_device(): after = lax.ppermute(first, TILE, [(j, i) for i, j in up])  4.13 us
    ppermute x1, starting transfers between devices, on_device(): before = lax.ppermute(last, TILE, up)  3.9 us
  transfers between devices with their start and end apart: 13, of which 6 were waited for; matrix products, arithmetic and copies ran while one was open for 4% of the time, Pallas kernels for 12%

profile of v4, /device:TPU:0, one launch (start us, length us, event | category | flops | bytes accessed | tf_op | source)
XLA Modules:
  0.0 62.3 jit_solution(9403978002481696699)
XLA Ops:
  0.0 4.5 %smooth_first.1 = (bf16[12,128,128]{2,1,0:T(8,128)(2,1)S(1)}, bf16[12,128,128]{2,1,0:T(8,128)(2,1)S(1)}, bf16[12,128,128]{2,1,0:T(8,128)(2,1)S(1)}, bf16[12,128,...) custom-call(bf16[2,1024,512]{2,1,0:T(8,128)(2,1)} %bitcast.3, ...), custom_call_target="tpu_custom_call" | custom-call | tf_op jit(solution)/shard_map/smooth_first/pallas_call | solution.py:206
  4.5 4.0 %collective-permute-start = (bf16[12,128,128]{2,1,0:T(8,128)(2,1)S(1)}, bf16[12,128,128]{2,1,0:T(8,128)(2,1)S(1)}, u32[]{:S(2)}, u32[]{:S(2)}) collective-permute-start(bf16[12,128,128]{2,1,0:T(8,128)(2,1)S(1)} %get-tuple-element.28), channel_id=1, source_target_pairs={{0,24},{4,28},{8,16},{12,20},{16,8},{20,12},{24,0},{28,4},{1,25},{... | collective-permute-start | bytes 1179656 | tf_op jit(solution)/shard_map/ppermute | solution.py:478
  9.2 3.9 %collective-permute-start.3 = (bf16[9,128,128]{2,1,0:T(8,128)(2,1)S(1)}, bf16[9,128,128]{2,1,0:T(8,128)(2,1)S(1)}, u32[]{:S(2)}, u32[]{:S(2)}) collective-permute-start(bf16[9,128,128]{2,1,0:T(8,128)(2,1)S(1)} %get-tuple-element.33), channel_id=1, source_target_pairs={{0,1},{1,2},{2,3},{4,5},{5,6},{6,7},{8,9},{9,10},{10,11},{12,13},{... | collective-permute-start | bytes 884744 | tf_op jit(solution)/shard_map/ppermute | solution.py:494
  13.1 1.3 %collective-permute-start.4 = (bf16[9,128,128]{2,1,0:T(8,128)(2,1)S(1)}, bf16[9,128,128]{2,1,0:T(8,128)(2,1)S(1)}, u32[]{:S(2)}, u32[]{:S(2)}) collective-permute-start(bf16[9,128,128]{2,1,0:T(8,128)(2,1)S(1)} %get-tuple-element.34), channel_id=1, source_target_pairs={{1,0},{2,1},{3,2},{5,4},{6,5},{7,6},{9,8},{10,9},{11,10},{13,12},{... | collective-permute-start | bytes 884744 | tf_op jit(solution)/shard_map/ppermute | solution.py:495
  14.4 1.3 %fusion.9 = (f32[256,128]{1,0:T(8,128)S(1)}, f32[256,128]{1,0:T(8,128)S(1)}) fusion(s32[256]{0:T(256)} %param.5), kind=kLoop, calls=%fused_computation.14 | loop fusion | flops 491520 | bytes 263168 | tf_op jit(solution)/shard_map/cos | solution.py:308
  15.7 0.8 %fusion.17 = (f32[256,8]{0,1:T(8,128)S(1)}, f32[256,8]{0,1:T(8,128)S(1)}) fusion(s32[8]{0:T(128)S(1)} %iota_multiply_fusion, s32[256]{0:T(256)} %param.5), kind=kLoop, calls=%fused_computation.27 | loop fusion | flops 28672 | bytes 17440 | tf_op jit(solution)/shard_map/cos | solution.py:308
  16.7 0.8 %filter_matrix.1 = (bf16[512,1024]{1,0:T(8,128)(2,1)S(1)}, bf16[512,1024]{1,0:T(8,128)(2,1)S(1)}) custom-call(f32[8,128]{1,0:T(8,128)S(1)} %convolution_multiply_fusion.wave_ref), custom_call_target="tpu_custom_call" | custom-call | tf_op jit(solution)/shard_map/filter_matrix/pallas_call | solution.py:318
  17.5 0.9 %collective-permute-done.3.before_ref = bf16[9,128,128]{2,1,0:T(8,128)(2,1)S(1)} collective-permute-done((bf16[9,128,128]{2,1,0:T(8,128)(2,1)S(1)}, bf16[9,128,128]{2,1,0:T(8,128)(2,1)S(1)}, u32[]{:S(2)}, u32[]{:S(2)}) %collective-permute-start.3) | collective-permute-done | bytes 294944 | tf_op jit(solution)/shard_map/ppermute | solution.py:494
  18.5 4.1 %collective-permute-done.4.after_ref = bf16[9,128,128]{2,1,0:T(8,128)(2,1)S(1)} collective-permute-done((bf16[9,128,128]{2,1,0:T(8,128)(2,1)S(1)}, bf16[9,128,128]{2,1,0:T(8,128)(2,1)S(1)}, u32[]{:S(2)}, u32[]{:S(2)}) %collective-permute-start.4) | collective-permute-done | bytes 294944 | tf_op jit(solution)/shard_map/ppermute | solution.py:495
  22.6 1.0 %smooth_rest.1 = (bf16[4,128,128]{2,1,0:T(8,128)(2,1)S(1)}, bf16[4,128,128]{2,1,0:T(8,128)(2,1)S(1)}, bf16[4,128,128]{2,1,0:T(8,128)(2,1)S(1)}, bf16[4,128,128]{2,1,0:T(8,128)(2,1)S(1)}) custom-call(bf16[3,1408,512]{2,1,0:T(8,128)(2,1)S(1)} %get-tuple-element.24.masked_ref, bf16[9,128,128]{2,1,0:T(8,128)(2,1)S(1)} %collective-permute-done.3.before_ref, ...), custom_call_target="tpu_custom_call" | custom-call | tf_op jit(solution)/shard_map/smooth_rest/pallas_call | solution.py:269
  23.6 1.1 %begin.1.refs_4_.refs_2_ = f32[512,1536]{1,0:T(8,128)S(1)} custom-call(bf16[512,1024]{1,0:T(8,128)(2,1)S(1)} %get-tuple-element.25.high_ref, bf16[512,1024]{1,0:T(8,128)(2,1)S(1)} %get-tuple-element.26.low_ref, bf16[12,128,128]{2,1,0:T(8,128)(2,1)S(1)} %get-tuple-element.27.refs_0_, bf16[12,128,128]{2,1,0:T(8,128)(2,1)S(1)} %collective-permute-done.refs_1_), custom_call_target="tpu_custom_call" | custom-call | tf_op jit(solution)/shard_map/begin/pallas_call | solution.py:365
  24.7 1.3 %collective-permute-done.1.refs_2_ = bf16[12,128,128]{2,1,0:T(8,128)(2,1)S(1)} collective-permute-done((bf16[12,128,128]{2,1,0:T(8,128)(2,1)S(1)}, bf16[12,128,128]{2,1,0:T(8,128)(2,1)S(1)}, u32[]{:S(2)}, u32[]{:S(2)}) %collective-permute-start.1) | collective-permute-done | bytes 393248 | tf_op jit(solution)/shard_map/ppermute | solution.py:478
  26.7 2.4 %collective-permute-start.9 = (bf16[4,128,128]{2,1,0:T(8,128)(2,1)S(1)}, bf16[4,128,128]{2,1,0:T(8,128)(2,1)S(1)}, u32[]{:S(2)}, u32[]{:S(2)}) collective-permute-start(bf16[4,128,128]{2,1,0:T(8,128)(2,1)S(1)} %get-tuple-element.40), channel_id=1, source_target_pairs={{0,24},{4,28},{8,16},{12,20},{16,8},{20,12},{24,0},{28,4},{1,25},{... | collective-permute-start | bytes 393224 | tf_op jit(solution)/shard_map/ppermute | solution.py:478
  29.1 0.6 collective-permute-start.10
  29.7 0.5 collective-permute-start.11
  30.2 2.6 %apply_filter.2 = (bf16[12,128,128]{2,1,0:T(8,128)(2,1)S(1)}, bf16[12,128,128]{2,1,0:T(8,128)(2,1)S(1)}, bf16[12,128,128]{2,1,0:T(8,128)(2,1)S(1)}, bf16[12,128,128]{2,1,0:T(8,128)(2,1)S(1)}) custom-call(bf16[512,1024]{1,0:T(8,128)(2,1)S(1)} %get-tuple-element.25.high_ref, bf16[512,1024]{1,0:T(8,128)(2,1)S(1)} %get-tuple-element.26.low_ref, ...), custom_call_target="tpu_custom_call" | custom-call | tf_op jit(solution)/shard_map/apply_filter/pallas_call | solution.py:397
  32.8 2.4 %collective-permute-start.6 = (bf16[12,128,128]{2,1,0:T(8,128)(2,1)S(1)}, bf16[12,128,128]{2,1,0:T(8,128)(2,1)S(1)}, u32[]{:S(2)}, u32[]{:S(2)}) collective-permute-start(bf16[12,128,128]{2,1,0:T(8,128)(2,1)S(1)} %get-tuple-element.37), channel_id=1, source_target_pairs={{0,24},{4,28},{8,16},{12,20},{16,8},{20,12},{24,0},{28,4},{1,25},{... | collective-permute-start | bytes 1179656 | tf_op jit(solution)/shard_map/ppermute | solution.py:478
  35.3 0.6 collective-permute-start.7
  36.5 4.6 %all_to_all.10.refs_0_ = bf16[2,512,512]{2,1,0:T(8,128)(2,1)S(1)} all-to-all(bf16[2,512,512]{2,1,0:T(8,128)(2,1)S(1)} %pack.3), channel_id=1, replica_groups={{0,4},{8,12},{16,20},{24,28},{1,5},{9,13},{17,21},{25,29},{2,6},{10,14}..., dimensions={0} | all-to-all | bytes 2097152 | tf_op jit(solution)/shard_map/all_to_all | solution.py:505
  41.1 2.1 %apply_filter.3 = bf16[4,4,128,128]{3,2,1,0:T(8,128)(2,1)} custom-call(bf16[512,1024]{1,0:T(8,128)(2,1)S(1)} %get-tuple-element.25.high_ref, bf16[512,1024]{1,0:T(8,128)(2,1)S(1)} %get-tuple-element.26.low_ref, bf16[2,512,512]{2,1,0:T(8,128)(2,1)S(1)} %all_to_all.10.refs_0_), custom_call_target="tpu_custom_call" | custom-call | tf_op jit(solution)/shard_map/apply_filter/pallas_call | solution.py:397
  43.2 3.6 %all-to-all-start.1 = ((bf16[4,4,128,128]{3,2,1,0:T(8,128)(2,1)}), bf16[4,4,128,128]{3,2,1,0:T(8,128)(2,1)S(1)}, u32[]{:S(2)}, u32[]{:S(2)}) async-start(bf16[4,4,128,128]{3,2,1,0:T(8,128)(2,1)} %apply_filter.3), calls=%async_computation.1 | async-start | bytes 1048576 | tf_op jit(solution)/shard_map/all_to_all | solution.py:508
  46.8 7.5 %collective-permute-done.7.refs_2_ = bf16[12,128,128]{2,1,0:T(8,128)(2,1)S(1)} collective-permute-done((bf16[12,128,128]{2,1,0:T(8,128)(2,1)S(1)}, bf16[12,128,128]{2,1,0:T(8,128)(2,1)S(1)}, u32[]{:S(2)}, u32[]{:S(2)}) %collective-permute-start.7) | collective-permute-done | bytes 393248 | tf_op jit(solution)/shard_map/ppermute | solution.py:478
  54.3 4.5 %all-to-all-done.1.refs_4_ = bf16[4,4,128,128]{3,2,1,0:T(8,128)(2,1)S(1)} async-done(((bf16[4,4,128,128]{3,2,1,0:T(8,128)(2,1)}), bf16[4,4,128,128]{3,2,1,0:T(8,128)(2,1)S(1)}, u32[]{:S(2)}, u32[]{:S(2)}) %all-to-all-start.1) | async-done | bytes 524320 | tf_op jit(solution)/shard_map/all_to_all | solution.py:508
  58.9 3.4 %anomaly.1 = f32[2,1024,512]{2,1,0:T(8,128)} custom-call(bf16[3,1408,512]{2,1,0:T(8,128)(2,1)} %copy-done, bf16[12,128,128]{2,1,0:T(8,128)(2,1)S(1)} %get-tuple-element.36.refs_4_.refs_0_, bf16[12,128,128]{2,1,0:T(8,128)(2,1)S(1)} %collective-permute-done.6.refs_1_, bf16[12,128,128]{2,1,0:T(8,128)(2,1)S(1)} %collective-permute-done.7.refs_2_, ...), custom_call_target="tpu_custom_call" | custom-call | tf_op jit(solution)/shard_map/anomaly/pallas_call | solution.py:458
  (19 shorter events, 2.2 us)
Async XLA Ops:
  4.5 20.2 %copy-start = (bf16[3,1408,512]{2,1,0:T(8,128)(2,1)}, bf16[3,1408,512]{2,1,0:T(8,128)(2,1)S(1)}, u32[]{:S(2)}) copy-start(bf16[3,1408,512]{2,1,0:T(8,128)(2,1)S(1)} %get-tuple-element.24.masked_ref) | copy-start | bytes 12976132
  4.5 19.1 %collective-permute-start = (bf16[12,128,128]{2,1,0:T(8,128)(2,1)S(1)}, bf16[12,128,128]{2,1,0:T(8,128)(2,1)S(1)}, u32[]{:S(2)}, u32[]{:S(2)}) collective-permute-start(bf16[12,128,128]{2,1,0:T(8,128)(2,1)S(1)} %get-tuple-element.28), channel_id=1, source_target_pairs={{0,24},{4,28},{8,16},{12,20},{16,8},{20,12},{24,0},{28,4},{1,25},{... | collective-permute-start | bytes 1179656 | tf_op jit(solution)/shard_map/ppermute | solution.py:478
  8.5 17.5 %collective-permute-start.1 = (bf16[12,128,128]{2,1,0:T(8,128)(2,1)S(1)}, bf16[12,128,128]{2,1,0:T(8,128)(2,1)S(1)}, u32[]{:S(2)}, u32[]{:S(2)}) collective-permute-start(bf16[12,128,128]{2,1,0:T(8,128)(2,1)S(1)} %get-tuple-element.29), channel_id=1, source_target_pairs={{0,16},{4,12},{8,24},{12,4},{16,0},{20,28},{24,8},{28,20},{1,17},{... | collective-permute-start | bytes 1179656 | tf_op jit(solution)/shard_map/ppermute | solution.py:478
  9.0 17.3 %collective-permute-start.2 = (bf16[12,128,128]{2,1,0:T(8,128)(2,1)S(1)}, bf16[12,128,128]{2,1,0:T(8,128)(2,1)S(1)}, u32[]{:S(2)}, u32[]{:S(2)}) collective-permute-start(bf16[12,128,128]{2,1,0:T(8,128)(2,1)S(1)} %get-tuple-element.30), channel_id=1, source_target_pairs={{0,8},{4,20},{8,0},{12,28},{16,24},{20,4},{24,16},{28,12},{1,9},{5... | collective-permute-start | bytes 1179656 | tf_op jit(solution)/shard_map/ppermute | solution.py:478
  9.2 9.3 %collective-permute-start.3 = (bf16[9,128,128]{2,1,0:T(8,128)(2,1)S(1)}, bf16[9,128,128]{2,1,0:T(8,128)(2,1)S(1)}, u32[]{:S(2)}, u32[]{:S(2)}) collective-permute-start(bf16[9,128,128]{2,1,0:T(8,128)(2,1)S(1)} %get-tuple-element.33), channel_id=1, source_target_pairs={{0,1},{1,2},{2,3},{4,5},{5,6},{6,7},{8,9},{9,10},{10,11},{12,13},{... | collective-permute-start | bytes 884744 | tf_op jit(solution)/shard_map/ppermute | solution.py:494
  13.1 9.5 %collective-permute-start.4 = (bf16[9,128,128]{2,1,0:T(8,128)(2,1)S(1)}, bf16[9,128,128]{2,1,0:T(8,128)(2,1)S(1)}, u32[]{:S(2)}, u32[]{:S(2)}) collective-permute-start(bf16[9,128,128]{2,1,0:T(8,128)(2,1)S(1)} %get-tuple-element.34), channel_id=1, source_target_pairs={{1,0},{2,1},{3,2},{5,4},{6,5},{7,6},{9,8},{10,9},{11,10},{13,12},{... | collective-permute-start | bytes 884744 | tf_op jit(solution)/shard_map/ppermute | solution.py:495
  26.6 3.6 %collective-permute-start.5 = (bf16[512,1536]{1,0:T(8,128)(2,1)S(1)}, bf16[512,1536]{1,0:T(8,128)(2,1)S(1)}, u32[]{:S(2)}, u32[]{:S(2)}) collective-permute-start(bf16[512,1536]{1,0:T(8,128)(2,1)S(1)} %pack.2.refs_0_), channel_id=1, source_target_pairs={{0,4},{4,0},{8,12},{12,8},{16,20},{20,16},{24,28},{28,24},{1,5},{5... | collective-permute-start | bytes 4718600 | tf_op jit(solution)/shard_map/ppermute | solution.py:501
  26.7 9.2 %collective-permute-start.9 = (bf16[4,128,128]{2,1,0:T(8,128)(2,1)S(1)}, bf16[4,128,128]{2,1,0:T(8,128)(2,1)S(1)}, u32[]{:S(2)}, u32[]{:S(2)}) collective-permute-start(bf16[4,128,128]{2,1,0:T(8,128)(2,1)S(1)} %get-tuple-element.40), channel_id=1, source_target_pairs={{0,24},{4,28},{8,16},{12,20},{16,8},{20,12},{24,0},{28,4},{1,25},{... | collective-permute-start | bytes 393224 | tf_op jit(solution)/shard_map/ppermute | solution.py:478
  29.1 7.3 %collective-permute-start.10 = (bf16[4,128,128]{2,1,0:T(8,128)(2,1)S(1)}, bf16[4,128,128]{2,1,0:T(8,128)(2,1)S(1)}, u32[]{:S(2)}, u32[]{:S(2)}) collective-permute-start(bf16[4,128,128]{2,1,0:T(8,128)(2,1)S(1)} %get-tuple-element.41), channel_id=1, source_target_pairs={{0,16},{4,12},{8,24},{12,4},{16,0},{20,28},{24,8},{28,20},{1,17},{... | collective-permute-start | bytes 393224 | tf_op jit(solution)/shard_map/ppermute | solution.py:478
  29.7 6.7 %collective-permute-start.11 = (bf16[4,128,128]{2,1,0:T(8,128)(2,1)S(1)}, bf16[4,128,128]{2,1,0:T(8,128)(2,1)S(1)}, u32[]{:S(2)}, u32[]{:S(2)}) collective-permute-start(bf16[4,128,128]{2,1,0:T(8,128)(2,1)S(1)} %get-tuple-element.42), channel_id=1, source_target_pairs={{0,8},{4,20},{8,0},{12,28},{16,24},{20,4},{24,16},{28,12},{1,9},{5... | collective-permute-start | bytes 393224 | tf_op jit(solution)/shard_map/ppermute | solution.py:478
  32.8 14.0 %collective-permute-start.6 = (bf16[12,128,128]{2,1,0:T(8,128)(2,1)S(1)}, bf16[12,128,128]{2,1,0:T(8,128)(2,1)S(1)}, u32[]{:S(2)}, u32[]{:S(2)}) collective-permute-start(bf16[12,128,128]{2,1,0:T(8,128)(2,1)S(1)} %get-tuple-element.37), channel_id=1, source_target_pairs={{0,24},{4,28},{8,16},{12,20},{16,8},{20,12},{24,0},{28,4},{1,25},{... | collective-permute-start | bytes 1179656 | tf_op jit(solution)/shard_map/ppermute | solution.py:478
  35.3 19.0 %collective-permute-start.7 = (bf16[12,128,128]{2,1,0:T(8,128)(2,1)S(1)}, bf16[12,128,128]{2,1,0:T(8,128)(2,1)S(1)}, u32[]{:S(2)}, u32[]{:S(2)}) collective-permute-start(bf16[12,128,128]{2,1,0:T(8,128)(2,1)S(1)} %get-tuple-element.38), channel_id=1, source_target_pairs={{0,16},{4,12},{8,24},{12,4},{16,0},{20,28},{24,8},{28,20},{1,17},{... | collective-permute-start | bytes 1179656 | tf_op jit(solution)/shard_map/ppermute | solution.py:478
  35.9 18.5 %collective-permute-start.8 = (bf16[12,128,128]{2,1,0:T(8,128)(2,1)S(1)}, bf16[12,128,128]{2,1,0:T(8,128)(2,1)S(1)}, u32[]{:S(2)}, u32[]{:S(2)}) collective-permute-start(bf16[12,128,128]{2,1,0:T(8,128)(2,1)S(1)} %get-tuple-element.39), channel_id=1, source_target_pairs={{0,8},{4,20},{8,0},{12,28},{16,24},{20,4},{24,16},{28,12},{1,9},{5... | collective-permute-start | bytes 1179656 | tf_op jit(solution)/shard_map/ppermute | solution.py:478
  43.2 15.7 %all-to-all-start.1 = ((bf16[4,4,128,128]{3,2,1,0:T(8,128)(2,1)}), bf16[4,4,128,128]{3,2,1,0:T(8,128)(2,1)S(1)}, u32[]{:S(2)}, u32[]{:S(2)}) async-start(bf16[4,4,128,128]{3,2,1,0:T(8,128)(2,1)} %apply_filter.3), calls=%async_computation.1 | async-start | bytes 1048576 | tf_op jit(solution)/shard_map/all_to_all | solution.py:508

commit v5 on v4

--- a/solution.py
+++ b/solution.py
@@ -113,8 +113,10 @@
 
 def smooth_lines(down, scale, lane):
     cols = down.shape[1]
-    west = jnp.where(lane == 0, 0.0, pltpu.roll(down, 1, 1))
-    east = jnp.where(lane == cols - 1, 0.0, pltpu.roll(down, cols - 1, 1))
+    west, east = pltpu.roll(down, 1, 1), pltpu.roll(down, cols - 1, 1)
+    lane = lane[:, :LANES]
+    west = jnp.concatenate([jnp.where(lane == 0, 0.0, west[:, :LANES]), west[:, LANES:]], axis=1)
+    east = jnp.concatenate([east[:, :-LANES], jnp.where(lane == LANES - 1, 0.0, east[:, -LANES:])], axis=1)
     return ((down + west + east) * scale).astype(jnp.bfloat16)
 
 

time: 62.6 us -> 62.6 us (level)
  transfers between devices with their start and end apart: 13 -> 13, of which waited for: 6 -> 6; matrix products, arithmetic and copies ran while one was open for 4% -> 4% of each run, Pallas kernels for 12% -> 13%
where the time goes in v5:
time: 62.6 us; the launch traced here: 62.3 us
  starting transfers between devices  20.6 us (33%)
  waiting for transfers between devices  18.6 us (30%)
  Pallas kernels  16 us (26%)
  blocking collectives  4.58 us (7%)
  other arithmetic  2.08 us (3%)
    ppermute x9, starting transfers between devices, exchange(): out[m] = lax.ppermute(pieces[m], DATE, to)  11.7 us
    ppermute x9, waiting for transfers between devices, exchange(): out[m] = lax.ppermute(pieces[m], DATE, to)  9.07 us
    pallas_call x2, Pallas kernels, apply_filter(): pl.pallas_call(functools.partial(apply_kernel, chips, shared, done), out_...  4.67 us
    all_to_all x1, blocking collectives, on_device(): lax.all_to_all(own, DATE, 0, 0, axis_index_groups=[[i, i + 1] for i in ra...  4.58 us
    all_to_all x1, waiting for transfers between devices, on_device(): results.append(lax.all_to_all(made, DATE, 0, 0, axis_index_groups=cores))  4.53 us
    pallas_call x1, Pallas kernels, smooth_first(): pl.pallas_call(functools.partial(first_kernel, chunks, chips), in_specs=[...  4.51 us
    ppermute x1, waiting for transfers between devices, on_device(): after = lax.ppermute(first, TILE, [(j, i) for i, j in up])  4.13 us
    ppermute x1, starting transfers between devices, on_device(): before = lax.ppermute(last, TILE, up)  3.9 us
  transfers between devices with their start and end apart: 13, of which 6 were waited for; matrix products, arithmetic and copies ran while one was open for 4% of the time, Pallas kernels for 13%

profile of v5, /device:TPU:0, one launch (start us, length us, event | category | flops | bytes accessed | tf_op | source)
XLA Modules:
  0.0 62.3 jit_solution(5638784444760691133)
XLA Ops:
  0.0 4.5 %smooth_first.1 = (bf16[12,128,128]{2,1,0:T(8,128)(2,1)S(1)}, bf16[12,128,128]{2,1,0:T(8,128)(2,1)S(1)}, bf16[12,128,128]{2,1,0:T(8,128)(2,1)S(1)}, bf16[12,128,...) custom-call(bf16[2,1024,512]{2,1,0:T(8,128)(2,1)} %bitcast.3, ...), custom_call_target="tpu_custom_call" | custom-call | tf_op jit(solution)/shard_map/smooth_first/pallas_call | solution.py:208
  4.5 4.0 %collective-permute-start = (bf16[12,128,128]{2,1,0:T(8,128)(2,1)S(1)}, bf16[12,128,128]{2,1,0:T(8,128)(2,1)S(1)}, u32[]{:S(2)}, u32[]{:S(2)}) collective-permute-start(bf16[12,128,128]{2,1,0:T(8,128)(2,1)S(1)} %get-tuple-element.28), channel_id=1, source_target_pairs={{0,24},{4,28},{8,16},{12,20},{16,8},{20,12},{24,0},{28,4},{1,25},{... | collective-permute-start | bytes 1179656 | tf_op jit(solution)/shard_map/ppermute | solution.py:480
  9.2 3.9 %collective-permute-start.3 = (bf16[9,128,128]{2,1,0:T(8,128)(2,1)S(1)}, bf16[9,128,128]{2,1,0:T(8,128)(2,1)S(1)}, u32[]{:S(2)}, u32[]{:S(2)}) collective-permute-start(bf16[9,128,128]{2,1,0:T(8,128)(2,1)S(1)} %get-tuple-element.33), channel_id=1, source_target_pairs={{0,1},{1,2},{2,3},{4,5},{5,6},{6,7},{8,9},{9,10},{10,11},{12,13},{... | collective-permute-start | bytes 884744 | tf_op jit(solution)/shard_map/ppermute | solution.py:496
  13.1 1.3 %collective-permute-start.4 = (bf16[9,128,128]{2,1,0:T(8,128)(2,1)S(1)}, bf16[9,128,128]{2,1,0:T(8,128)(2,1)S(1)}, u32[]{:S(2)}, u32[]{:S(2)}) collective-permute-start(bf16[9,128,128]{2,1,0:T(8,128)(2,1)S(1)} %get-tuple-element.34), channel_id=1, source_target_pairs={{1,0},{2,1},{3,2},{5,4},{6,5},{7,6},{9,8},{10,9},{11,10},{13,12},{... | collective-permute-start | bytes 884744 | tf_op jit(solution)/shard_map/ppermute | solution.py:497
  14.4 1.3 %fusion.9 = (f32[256,128]{1,0:T(8,128)S(1)}, f32[256,128]{1,0:T(8,128)S(1)}) fusion(s32[256]{0:T(256)} %param.5), kind=kLoop, calls=%fused_computation.14 | loop fusion | flops 491520 | bytes 263168 | tf_op jit(solution)/shard_map/cos | solution.py:310
  15.7 0.8 %fusion.17 = (f32[256,8]{0,1:T(8,128)S(1)}, f32[256,8]{0,1:T(8,128)S(1)}) fusion(s32[8]{0:T(128)S(1)} %iota_multiply_fusion, s32[256]{0:T(256)} %param.5), kind=kLoop, calls=%fused_computation.27 | loop fusion | flops 28672 | bytes 17440 | tf_op jit(solution)/shard_map/cos | solution.py:310
  16.7 0.8 %filter_matrix.1 = (bf16[512,1024]{1,0:T(8,128)(2,1)S(1)}, bf16[512,1024]{1,0:T(8,128)(2,1)S(1)}) custom-call(f32[8,128]{1,0:T(8,128)S(1)} %convolution_multiply_fusion.wave_ref), custom_call_target="tpu_custom_call" | custom-call | tf_op jit(solution)/shard_map/filter_matrix/pallas_call | solution.py:320
  17.6 0.9 %collective-permute-done.3.before_ref = bf16[9,128,128]{2,1,0:T(8,128)(2,1)S(1)} collective-permute-done((bf16[9,128,128]{2,1,0:T(8,128)(2,1)S(1)}, bf16[9,128,128]{2,1,0:T(8,128)(2,1)S(1)}, u32[]{:S(2)}, u32[]{:S(2)}) %collective-permute-start.3) | collective-permute-done | bytes 294944 | tf_op jit(solution)/shard_map/ppermute | solution.py:496
  18.5 4.1 %collective-permute-done.4.after_ref = bf16[9,128,128]{2,1,0:T(8,128)(2,1)S(1)} collective-permute-done((bf16[9,128,128]{2,1,0:T(8,128)(2,1)S(1)}, bf16[9,128,128]{2,1,0:T(8,128)(2,1)S(1)}, u32[]{:S(2)}, u32[]{:S(2)}) %collective-permute-start.4) | collective-permute-done | bytes 294944 | tf_op jit(solution)/shard_map/ppermute | solution.py:497
  22.6 1.0 %smooth_rest.1 = (bf16[4,128,128]{2,1,0:T(8,128)(2,1)S(1)}, bf16[4,128,128]{2,1,0:T(8,128)(2,1)S(1)}, bf16[4,128,128]{2,1,0:T(8,128)(2,1)S(1)}, bf16[4,128,128]{2,1,0:T(8,128)(2,1)S(1)}) custom-call(bf16[3,1408,512]{2,1,0:T(8,128)(2,1)S(1)} %get-tuple-element.24.masked_ref, bf16[9,128,128]{2,1,0:T(8,128)(2,1)S(1)} %collective-permute-done.3.before_ref, ...), custom_call_target="tpu_custom_call" | custom-call | tf_op jit(solution)/shard_map/smooth_rest/pallas_call | solution.py:271
  23.6 1.1 %begin.1.refs_4_.refs_2_ = f32[512,1536]{1,0:T(8,128)S(1)} custom-call(bf16[512,1024]{1,0:T(8,128)(2,1)S(1)} %get-tuple-element.25.high_ref, bf16[512,1024]{1,0:T(8,128)(2,1)S(1)} %get-tuple-element.26.low_ref, bf16[12,128,128]{2,1,0:T(8,128)(2,1)S(1)} %get-tuple-element.27.refs_0_, bf16[12,128,128]{2,1,0:T(8,128)(2,1)S(1)} %collective-permute-done.refs_1_), custom_call_target="tpu_custom_call" | custom-call | tf_op jit(solution)/shard_map/begin/pallas_call | solution.py:367
  24.7 1.3 %collective-permute-done.1.refs_2_ = bf16[12,128,128]{2,1,0:T(8,128)(2,1)S(1)} collective-permute-done((bf16[12,128,128]{2,1,0:T(8,128)(2,1)S(1)}, bf16[12,128,128]{2,1,0:T(8,128)(2,1)S(1)}, u32[]{:S(2)}, u32[]{:S(2)}) %collective-permute-start.1) | collective-permute-done | bytes 393248 | tf_op jit(solution)/shard_map/ppermute | solution.py:480
  26.7 2.4 %collective-permute-start.9 = (bf16[4,128,128]{2,1,0:T(8,128)(2,1)S(1)}, bf16[4,128,128]{2,1,0:T(8,128)(2,1)S(1)}, u32[]{:S(2)}, u32[]{:S(2)}) collective-permute-start(bf16[4,128,128]{2,1,0:T(8,128)(2,1)S(1)} %get-tuple-element.40), channel_id=1, source_target_pairs={{0,24},{4,28},{8,16},{12,20},{16,8},{20,12},{24,0},{28,4},{1,25},{... | collective-permute-start | bytes 393224 | tf_op jit(solution)/shard_map/ppermute | solution.py:480
  29.1 0.6 collective-permute-start.10
  30.2 2.6 %apply_filter.2 = (bf16[12,128,128]{2,1,0:T(8,128)(2,1)S(1)}, bf16[12,128,128]{2,1,0:T(8,128)(2,1)S(1)}, bf16[12,128,128]{2,1,0:T(8,128)(2,1)S(1)}, bf16[12,128,128]{2,1,0:T(8,128)(2,1)S(1)}) custom-call(bf16[512,1024]{1,0:T(8,128)(2,1)S(1)} %get-tuple-element.25.high_ref, bf16[512,1024]{1,0:T(8,128)(2,1)S(1)} %get-tuple-element.26.low_ref, ...), custom_call_target="tpu_custom_call" | custom-call | tf_op jit(solution)/shard_map/apply_filter/pallas_call | solution.py:399
  32.8 2.4 %collective-permute-start.6 = (bf16[12,128,128]{2,1,0:T(8,128)(2,1)S(1)}, bf16[12,128,128]{2,1,0:T(8,128)(2,1)S(1)}, u32[]{:S(2)}, u32[]{:S(2)}) collective-permute-start(bf16[12,128,128]{2,1,0:T(8,128)(2,1)S(1)} %get-tuple-element.37), channel_id=1, source_target_pairs={{0,24},{4,28},{8,16},{12,20},{16,8},{20,12},{24,0},{28,4},{1,25},{... | collective-permute-start | bytes 1179656 | tf_op jit(solution)/shard_map/ppermute | solution.py:480
  35.3 0.6 collective-permute-start.7
  35.9 0.5 collective-permute-start.8
  36.6 4.6 %all_to_all.10.refs_0_ = bf16[2,512,512]{2,1,0:T(8,128)(2,1)S(1)} all-to-all(bf16[2,512,512]{2,1,0:T(8,128)(2,1)S(1)} %pack.3), channel_id=1, replica_groups={{0,4},{8,12},{16,20},{24,28},{1,5},{9,13},{17,21},{25,29},{2,6},{10,14}..., dimensions={0} | all-to-all | bytes 2097152 | tf_op jit(solution)/shard_map/all_to_all | solution.py:507
  41.1 2.1 %apply_filter.3 = bf16[4,4,128,128]{3,2,1,0:T(8,128)(2,1)} custom-call(bf16[512,1024]{1,0:T(8,128)(2,1)S(1)} %get-tuple-element.25.high_ref, bf16[512,1024]{1,0:T(8,128)(2,1)S(1)} %get-tuple-element.26.low_ref, bf16[2,512,512]{2,1,0:T(8,128)(2,1)S(1)} %all_to_all.10.refs_0_), custom_call_target="tpu_custom_call" | custom-call | tf_op jit(solution)/shard_map/apply_filter/pallas_call | solution.py:399
  43.2 3.6 %all-to-all-start.1 = ((bf16[4,4,128,128]{3,2,1,0:T(8,128)(2,1)}), bf16[4,4,128,128]{3,2,1,0:T(8,128)(2,1)S(1)}, u32[]{:S(2)}, u32[]{:S(2)}) async-start(bf16[4,4,128,128]{3,2,1,0:T(8,128)(2,1)} %apply_filter.3), calls=%async_computation.1 | async-start | bytes 1048576 | tf_op jit(solution)/shard_map/all_to_all | solution.py:510
  46.8 7.5 %collective-permute-done.7.refs_2_ = bf16[12,128,128]{2,1,0:T(8,128)(2,1)S(1)} collective-permute-done((bf16[12,128,128]{2,1,0:T(8,128)(2,1)S(1)}, bf16[12,128,128]{2,1,0:T(8,128)(2,1)S(1)}, u32[]{:S(2)}, u32[]{:S(2)}) %collective-permute-start.7) | collective-permute-done | bytes 393248 | tf_op jit(solution)/shard_map/ppermute | solution.py:480
  54.3 4.5 %all-to-all-done.1.refs_4_ = bf16[4,4,128,128]{3,2,1,0:T(8,128)(2,1)S(1)} async-done(((bf16[4,4,128,128]{3,2,1,0:T(8,128)(2,1)}), bf16[4,4,128,128]{3,2,1,0:T(8,128)(2,1)S(1)}, u32[]{:S(2)}, u32[]{:S(2)}) %all-to-all-start.1) | async-done | bytes 524320 | tf_op jit(solution)/shard_map/all_to_all | solution.py:510
  58.9 3.4 %anomaly.1 = f32[2,1024,512]{2,1,0:T(8,128)} custom-call(bf16[3,1408,512]{2,1,0:T(8,128)(2,1)} %copy-done, bf16[12,128,128]{2,1,0:T(8,128)(2,1)S(1)} %get-tuple-element.36.refs_4_.refs_0_, bf16[12,128,128]{2,1,0:T(8,128)(2,1)S(1)} %collective-permute-done.6.refs_1_, bf16[12,128,128]{2,1,0:T(8,128)(2,1)S(1)} %collective-permute-done.7.refs_2_, ...), custom_call_target="tpu_custom_call" | custom-call | tf_op jit(solution)/shard_map/anomaly/pallas_call | solution.py:460
  (19 shorter events, 2.2 us)
Async XLA Ops:
  4.5 20.2 %copy-start = (bf16[3,1408,512]{2,1,0:T(8,128)(2,1)}, bf16[3,1408,512]{2,1,0:T(8,128)(2,1)S(1)}, u32[]{:S(2)}) copy-start(bf16[3,1408,512]{2,1,0:T(8,128)(2,1)S(1)} %get-tuple-element.24.masked_ref) | copy-start | bytes 12976132
  4.5 19.1 %collective-permute-start = (bf16[12,128,128]{2,1,0:T(8,128)(2,1)S(1)}, bf16[12,128,128]{2,1,0:T(8,128)(2,1)S(1)}, u32[]{:S(2)}, u32[]{:S(2)}) collective-permute-start(bf16[12,128,128]{2,1,0:T(8,128)(2,1)S(1)} %get-tuple-element.28), channel_id=1, source_target_pairs={{0,24},{4,28},{8,16},{12,20},{16,8},{20,12},{24,0},{28,4},{1,25},{... | collective-permute-start | bytes 1179656 | tf_op jit(solution)/shard_map/ppermute | solution.py:480
  8.5 17.5 %collective-permute-start.1 = (bf16[12,128,128]{2,1,0:T(8,128)(2,1)S(1)}, bf16[12,128,128]{2,1,0:T(8,128)(2,1)S(1)}, u32[]{:S(2)}, u32[]{:S(2)}) collective-permute-start(bf16[12,128,128]{2,1,0:T(8,128)(2,1)S(1)} %get-tuple-element.29), channel_id=1, source_target_pairs={{0,16},{4,12},{8,24},{12,4},{16,0},{20,28},{24,8},{28,20},{1,17},{... | collective-permute-start | bytes 1179656 | tf_op jit(solution)/shard_map/ppermute | solution.py:480
  9.0 17.3 %collective-permute-start.2 = (bf16[12,128,128]{2,1,0:T(8,128)(2,1)S(1)}, bf16[12,128,128]{2,1,0:T(8,128)(2,1)S(1)}, u32[]{:S(2)}, u32[]{:S(2)}) collective-permute-start(bf16[12,128,128]{2,1,0:T(8,128)(2,1)S(1)} %get-tuple-element.30), channel_id=1, source_target_pairs={{0,8},{4,20},{8,0},{12,28},{16,24},{20,4},{24,16},{28,12},{1,9},{5... | collective-permute-start | bytes 1179656 | tf_op jit(solution)/shard_map/ppermute | solution.py:480
  9.2 9.3 %collective-permute-start.3 = (bf16[9,128,128]{2,1,0:T(8,128)(2,1)S(1)}, bf16[9,128,128]{2,1,0:T(8,128)(2,1)S(1)}, u32[]{:S(2)}, u32[]{:S(2)}) collective-permute-start(bf16[9,128,128]{2,1,0:T(8,128)(2,1)S(1)} %get-tuple-element.33), channel_id=1, source_target_pairs={{0,1},{1,2},{2,3},{4,5},{5,6},{6,7},{8,9},{9,10},{10,11},{12,13},{... | collective-permute-start | bytes 884744 | tf_op jit(solution)/shard_map/ppermute | solution.py:496
  13.1 9.5 %collective-permute-start.4 = (bf16[9,128,128]{2,1,0:T(8,128)(2,1)S(1)}, bf16[9,128,128]{2,1,0:T(8,128)(2,1)S(1)}, u32[]{:S(2)}, u32[]{:S(2)}) collective-permute-start(bf16[9,128,128]{2,1,0:T(8,128)(2,1)S(1)} %get-tuple-element.34), channel_id=1, source_target_pairs={{1,0},{2,1},{3,2},{5,4},{6,5},{7,6},{9,8},{10,9},{11,10},{13,12},{... | collective-permute-start | bytes 884744 | tf_op jit(solution)/shard_map/ppermute | solution.py:497
  26.6 3.6 %collective-permute-start.5 = (bf16[512,1536]{1,0:T(8,128)(2,1)S(1)}, bf16[512,1536]{1,0:T(8,128)(2,1)S(1)}, u32[]{:S(2)}, u32[]{:S(2)}) collective-permute-start(bf16[512,1536]{1,0:T(8,128)(2,1)S(1)} %pack.2.refs_0_), channel_id=1, source_target_pairs={{0,4},{4,0},{8,12},{12,8},{16,20},{20,16},{24,28},{28,24},{1,5},{5... | collective-permute-start | bytes 4718600 | tf_op jit(solution)/shard_map/ppermute | solution.py:503
  26.7 9.2 %collective-permute-start.9 = (bf16[4,128,128]{2,1,0:T(8,128)(2,1)S(1)}, bf16[4,128,128]{2,1,0:T(8,128)(2,1)S(1)}, u32[]{:S(2)}, u32[]{:S(2)}) collective-permute-start(bf16[4,128,128]{2,1,0:T(8,128)(2,1)S(1)} %get-tuple-element.40), channel_id=1, source_target_pairs={{0,24},{4,28},{8,16},{12,20},{16,8},{20,12},{24,0},{28,4},{1,25},{... | collective-permute-start | bytes 393224 | tf_op jit(solution)/shard_map/ppermute | solution.py:480
  29.1 7.3 %collective-permute-start.10 = (bf16[4,128,128]{2,1,0:T(8,128)(2,1)S(1)}, bf16[4,128,128]{2,1,0:T(8,128)(2,1)S(1)}, u32[]{:S(2)}, u32[]{:S(2)}) collective-permute-start(bf16[4,128,128]{2,1,0:T(8,128)(2,1)S(1)} %get-tuple-element.41), channel_id=1, source_target_pairs={{0,16},{4,12},{8,24},{12,4},{16,0},{20,28},{24,8},{28,20},{1,17},{... | collective-permute-start | bytes 393224 | tf_op jit(solution)/shard_map/ppermute | solution.py:480
  29.7 6.7 %collective-permute-start.11 = (bf16[4,128,128]{2,1,0:T(8,128)(2,1)S(1)}, bf16[4,128,128]{2,1,0:T(8,128)(2,1)S(1)}, u32[]{:S(2)}, u32[]{:S(2)}) collective-permute-start(bf16[4,128,128]{2,1,0:T(8,128)(2,1)S(1)} %get-tuple-element.42), channel_id=1, source_target_pairs={{0,8},{4,20},{8,0},{12,28},{16,24},{20,4},{24,16},{28,12},{1,9},{5... | collective-permute-start | bytes 393224 | tf_op jit(solution)/shard_map/ppermute | solution.py:480
  32.8 14.0 %collective-permute-start.6 = (bf16[12,128,128]{2,1,0:T(8,128)(2,1)S(1)}, bf16[12,128,128]{2,1,0:T(8,128)(2,1)S(1)}, u32[]{:S(2)}, u32[]{:S(2)}) collective-permute-start(bf16[12,128,128]{2,1,0:T(8,128)(2,1)S(1)} %get-tuple-element.37), channel_id=1, source_target_pairs={{0,24},{4,28},{8,16},{12,20},{16,8},{20,12},{24,0},{28,4},{1,25},{... | collective-permute-start | bytes 1179656 | tf_op jit(solution)/shard_map/ppermute | solution.py:480
  35.3 19.0 %collective-permute-start.7 = (bf16[12,128,128]{2,1,0:T(8,128)(2,1)S(1)}, bf16[12,128,128]{2,1,0:T(8,128)(2,1)S(1)}, u32[]{:S(2)}, u32[]{:S(2)}) collective-permute-start(bf16[12,128,128]{2,1,0:T(8,128)(2,1)S(1)} %get-tuple-element.38), channel_id=1, source_target_pairs={{0,16},{4,12},{8,24},{12,4},{16,0},{20,28},{24,8},{28,20},{1,17},{... | collective-permute-start | bytes 1179656 | tf_op jit(solution)/shard_map/ppermute | solution.py:480
  35.9 18.5 %collective-permute-start.8 = (bf16[12,128,128]{2,1,0:T(8,128)(2,1)S(1)}, bf16[12,128,128]{2,1,0:T(8,128)(2,1)S(1)}, u32[]{:S(2)}, u32[]{:S(2)}) collective-permute-start(bf16[12,128,128]{2,1,0:T(8,128)(2,1)S(1)} %get-tuple-element.39), channel_id=1, source_target_pairs={{0,8},{4,20},{8,0},{12,28},{16,24},{20,4},{24,16},{28,12},{1,9},{5... | collective-permute-start | bytes 1179656 | tf_op jit(solution)/shard_map/ppermute | solution.py:480
  43.2 15.7 %all-to-all-start.1 = ((bf16[4,4,128,128]{3,2,1,0:T(8,128)(2,1)}), bf16[4,4,128,128]{3,2,1,0:T(8,128)(2,1)S(1)}, u32[]{:S(2)}, u32[]{:S(2)}) async-start(bf16[4,4,128,128]{3,2,1,0:T(8,128)(2,1)} %apply_filter.3), calls=%async_computation.1 | async-start | bytes 1048576 | tf_op jit(solution)/shard_map/all_to_all | solution.py:510
